TPU v7x, 256 devices: a whole 4x4x8 slice. The times are simulated.
256 devices in a mesh: dp: 32 (over z, y_hi, core), tensor: 8 (over y_lo, x).
Axes of the slice: x: 4, y: 4 (y_hi: 2, y_lo: 2; y = y_hi * 2 + y_lo), z: 8, core: 2. Of those that a mesh axis runs over, the one named last changes fastest.
Arguments:
- image_feat: bfloat16 [16384, 1152], P('dp', 'tensor'), as said below
- text_feat: bfloat16 [16384, 1152], P('dp', 'tensor'), as said below
- image_head: bfloat16 [1152, 1152], P('tensor'), may hold values from -0.1875 to 0.1875
- text_head: bfloat16 [1152, 1152], P('tensor'), may hold values from -0.1875 to 0.1875
- logit_scale: float32 [1], replicated, may hold values from 4 to 12
- logit_bias: float32 [1], replicated, may hold values from -4 to -1
Outputs:
- grad_image_head: float32 [1152, 1152], P('tensor')
- grad_text_head: float32 [1152, 1152], P('tensor')
- row_loss: float32 [16384], P('dp')
Inputs may be any that keep to these rules, and one draw needn't show every extreme that they name: `image_feat`: feature rows and columns have different scales. `text_feat`: feature rows and columns have different scales.
All inputs are finite; a program needn't handle non-finite values.
Results may differ from a plain program's by a relative error of at most 0.0065.
Values may be sent and summed in bfloat16 or wider, within the bound.
No kernel may reach another device: no remote copies, remote signals or barrier semaphores. Data moves between devices by JAX's collectives and lax.ppermute only.
A program may use at most 64 MiB of HBM per device.

v0:
```python
import math

import jax
import jax.numpy as jnp
from jax import lax
from jax.sharding import PartitionSpec as P


def unit(raw):
    width = raw.shape[-1]
    mean_sq = jnp.mean(raw * raw, axis=-1, keepdims=True)
    return raw * lax.rsqrt(mean_sq + 1e-06) / math.sqrt(width)


def back(raw, grad):
    width = raw.shape[-1]
    mean_sq = jnp.mean(raw * raw, axis=-1, keepdims=True)
    factor = lax.rsqrt(mean_sq + 1e-06) / math.sqrt(width)
    inner = jnp.sum(grad * raw, axis=-1, keepdims=True)
    return factor * grad - raw * factor * inner / (width * (mean_sq + 1e-06))


def contract_rows(left, right):
    return lax.dot_general(
        left, right, (((0,), (0,)), ((), ())), preferred_element_type=jnp.float32
    )


def contract_cols(left, right):
    return lax.dot_general(
        left, right, (((1,), (1,)), ((), ())), preferred_element_type=jnp.float32
    )


def on_device(image_feat, text_feat, image_head, text_head, logit_scale, logit_bias):
    pairs = image_feat.shape[0]
    n_data = lax.axis_size("dp")
    batch = pairs * n_data
    coef = logit_scale[0] * (1.0 / math.sqrt(batch))
    image_part = jnp.dot(image_feat, image_head, preferred_element_type=jnp.float32)
    text_part = jnp.dot(text_feat, text_head, preferred_element_type=jnp.float32)
    image_raw = lax.psum(image_part, "tensor")
    text_raw = lax.psum_scatter(text_part, "tensor", scatter_dimension=0, tiled=True)
    image_unit = unit(image_raw).astype(jnp.bfloat16)
    text_unit = unit(text_raw).astype(jnp.bfloat16)
    rows_own = text_unit.shape[0]
    my_data = lax.axis_index("dp")
    my_tensor = lax.axis_index("tensor")
    image_global = my_data * pairs + jnp.arange(pairs, dtype=jnp.int32)
    piece = lax.all_gather(text_unit, "dp", axis=0, tiled=True)
    local = jnp.arange(piece.shape[0], dtype=jnp.int32)
    text_global = local // rows_own * pairs + my_tensor * rows_own + local % rows_own
    scores = logit_scale[0] * contract_cols(image_unit, piece) + logit_bias[0]
    match = (image_global[:, None] == text_global[None, :]).astype(jnp.float32)
    weight = (jax.nn.sigmoid(scores) - match).astype(jnp.bfloat16)
    losses = jnp.sum(jax.nn.softplus(scores) - match * scores, axis=1)
    weight, losses = (weight, losses)
    image_grad = coef * jnp.dot(weight, piece, preferred_element_type=jnp.float32)
    term = coef * contract_rows(weight, image_unit)
    image_grad, loss_sum, text_terms = (image_grad, losses, term)
    text_grad = lax.psum_scatter(
        text_terms.astype(jnp.bfloat16), "dp", scatter_dimension=0, tiled=True
    ).astype(jnp.float32)
    image_grad, loss_sum = lax.psum((image_grad, loss_sum), "tensor")
    row_loss = loss_sum / batch
    image_back = back(image_raw, image_grad).astype(jnp.bfloat16)
    text_back = back(text_raw, text_grad).astype(jnp.bfloat16)
    group_back = lax.all_gather(text_back, "tensor", axis=0, tiled=True)
    image_slice = contract_rows(image_feat, image_back)
    text_slice = contract_rows(text_feat, group_back)
    grad_image_head, grad_text_head = lax.psum((image_slice, text_slice), "dp")
    return (grad_image_head, grad_text_head, row_loss)


def solution(mesh):
    placed = (P("dp", "tensor"), P("dp", "tensor"), P("tensor", None), P("tensor", None), P(), P())
    return jax.shard_map(
        on_device,
        mesh=mesh,
        in_specs=placed,
        out_specs=(P("tensor", None), P("tensor", None), P("dp")),
        check_vma=False,
    )
```

profile of v0, /device:TPU:1, one launch (start us, length us, event | category | flops | bytes accessed | tf_op | source)
XLA Modules:
  0.0 800.6 jit_solution(17769966321114936079)
XLA Ops:
  7.2 0.0 copy-start
  7.2 0.0 copy-start.6
  7.2 0.0 copy-start.5
  7.2 0.0 reduce-scatter.3.cloned.1.call-start
  7.2 0.9 copy-done
  8.1 2.9 fusion.25
  11.0 0.0 reduce-scatter.3.cloned.1.call-update
  11.1 0.0 all-reduce.5.cloned.1.call-start
  11.1 0.0 copy-done.6
  11.1 0.0 copy-done.5
  11.1 2.0 fusion.24
  13.2 0.0 all-reduce.5.cloned.1.call-update
  13.2 0.0 all-gather.3.cloned.1.call-start
  13.2 42.8 %reduce-scatter.3.cloned.1.call-done = f32[64,1152]{1,0:T(8,128)} async-done(((f32[512,1152]{1,0:T(8,128)}), f32[64,1152]{1,0:T(8,128)}) %reduce-scatter.3.cloned.1.call-update) | async-done | bytes 294928 | tf_op jit(solution)/shard_map/reduce_scatter | solution.py:43
  56.0 1.1 multiply_reduce_fusion.2
  57.1 1.7 multiply_convert_fusion.1
  58.8 0.0 all-gather.3.cloned.1.call-update
  58.9 0.0 reduce-scatter.5.cloned.1.call-start
  60.2 89.0 %all-reduce.5.cloned.1.call-done = f32[512,1152]{1,0:T(8,128)} async-done(((f32[512,1152]{1,0:T(8,128)}), f32[512,1152]{1,0:T(8,128)}) %all-reduce.5.cloned.1.call-update) | async-done | bytes 2359312 | tf_op jit(solution)/shard_map/psum | solution.py:42
  149.3 1.9 multiply_reduce_fusion.1
  151.2 94.2 %all-gather.3.cloned.1.call-done = bf16[2048,1152]{1,0:T(8,128)(2,1)} async-done(((bf16[64,1152]{1,0:T(8,128)(2,1)}), bf16[2048,1152]{1,0:T(8,128)(2,1)}) %all-gather.3.cloned.1.call-update) | async-done | bytes 4718608 | tf_op jit(solution)/shard_map/all_gather | solution.py:50
  245.4 7.8 fusion.4
  253.1 2.1 copy-done.7
  255.2 0.0 copy-done.1
  255.2 5.4 fusion
  260.6 0.0 reduce-scatter.5.cloned.1.call-update
  260.6 0.0 all-reduce.7.cloned.1.call-start
  260.7 0.0 copy-start.2
  260.7 8.7 %convolution_multiply_fusion.1 = f32[512,1152]{1,0:T(8,128)} fusion(bf16[2048,1152]{1,0:T(8,128)(2,1)} %all-gather.3.cloned.1.call-done, f32[]{:T(128)S(6)} %mul.132, f32[512,2048]{1,0:T(8,128)} %copy-done.7, s32[2048]{0:T(1024)S(1)} %fusion.16, f32[]{:T(128)} %bitcast.19, f32[]{:T(128)} %bitcast.16, s32[512]{0:T(512)S(1)} %iota_add_fusion), kind=kOutput, calls=%fused_computation.10 | convolution fusion | flops 2425946112 | bytes 11282444 | tf_op jit(solution)/shard_map/dot_general | solution.py:58
  269.4 0.0 all-reduce.7.cloned.1.call-update
  269.4 0.0 all-gather.5.cloned.1.call-start
  269.4 114.3 %reduce-scatter.5.cloned.1.call-done = bf16[64,1152]{1,0:T(8,128)(2,1)} async-done(((bf16[2048,1152]{1,0:T(8,128)(2,1)}), bf16[64,1152]{1,0:T(8,128)(2,1)}) %reduce-scatter.5.cloned.1.call-update) | async-done | bytes 147472 | tf_op jit(solution)/shard_map/reduce_scatter | solution.py:61
  383.7 1.0 fusion.7
  384.8 1.7 fusion.6
  386.5 0.0 all-gather.5.cloned.1.call-update
  386.5 0.0 all-reduce.9.cloned.1.call-start
  386.6 87.7 %all-reduce.7.cloned.1.call-done = f32[512,1152]{1,0:T(8,128)} async-done(((f32[512,1152]{1,0:T(8,128)}), f32[512,1152]{1,0:T(8,128)}) %all-reduce.7.cloned.1.call-update) | async-done | bytes 2359312 | tf_op jit(solution)/shard_map/psum | solution.py:64
  474.3 2.1 multiply_reduce_fusion
  476.4 0.2 copy-done.3
  476.7 1.7 convolution_bitcast_fusion.1
  478.4 38.8 %all-gather.5.cloned.1.call-done = bf16[512,1152]{1,0:T(8,128)(2,1)} async-done(((bf16[64,1152]{1,0:T(8,128)(2,1)}), bf16[512,1152]{1,0:T(8,128)(2,1)}) %all-gather.5.cloned.1.call-update) | async-done | bytes 1179664 | tf_op jit(solution)/shard_map/all_gather | solution.py:68
  517.2 2.5 convolution_bitcast_fusion
  519.7 0.0 all-reduce.9.cloned.1.call-update
  519.7 15.0 %psum.39 = f32[512]{0:T(512)S(1)} all-reduce(f32[512]{0:T(512)S(1)} %get-tuple-element.11), channel_id=1, replica_groups=mesh['dp'=32,'tensor'=8] {'tensor'}, use_global_device_ids=true, to_apply=%region_11.12 | all-reduce | flops 512 | bytes 4096 | tf_op jit(solution)/shard_map/psum | solution.py:64
  534.7 0.6 broadcast_multiply_fusion
  535.3 254.5 %all-reduce.9.cloned.1.call-done = (f32[144,1152]{1,0:T(8,128)}, f32[144,1152]{1,0:T(8,128)}) async-done(((f32[144,1152]{1,0:T(8,128)}, f32[144,1152]{1,0:T(8,128)}), (f32[144,1152]{1,0:T(8,128)}, f32[144,1152]{1,0:T(8,128)})) %all-reduce.9.cloned.1.call-update) | async-done | bytes 1327120 | tf_op jit(solution)/shard_map/psum | solution.py:71
  789.8 2.0 copy.15
  791.7 2.0 copy.16
  (10 shorter events, 0.0 us)
Async XLA Ops:
  7.2 1.0 copy-start
  7.2 3.9 copy-start.6
  7.2 3.9 copy-start.5
  7.2 48.8 %reduce-scatter.3.cloned.1.call-start = ((), (), s32[]{:S(2)}) async-start(), calls=%async_computation.3 | async-start | bytes 2654208 | tf_op jit(solution)/shard_map/reduce_scatter | solution.py:43
  11.1 138.2 %all-reduce.5.cloned.1.call-start = ((), (), s32[]{:S(2)}) async-start(), calls=%async_computation.2 | async-start | bytes 4718592 | tf_op jit(solution)/shard_map/psum | solution.py:42
  13.2 232.2 %all-gather.3.cloned.1.call-start = ((), (), s32[]{:S(2)}) async-start(), calls=%async_computation.4 | async-start | bytes 4866048 | tf_op jit(solution)/shard_map/all_gather | solution.py:50
  58.9 324.9 %reduce-scatter.5.cloned.1.call-start = ((), (), s32[]{:S(2)}) async-start(), calls=%async_computation.6 | async-start | bytes 4866048 | tf_op jit(solution)/shard_map/reduce_scatter | solution.py:61
  245.4 9.8 %copy-start.1 = (f32[512,1152]{1,0:T(8,128)S(1)}, f32[512,1152]{1,0:T(8,128)}, u32[]{:S(2)}) copy-start(f32[512,1152]{1,0:T(8,128)} %all-reduce.5.cloned.1.call-done) | copy-start | bytes 7077892
  253.1 2.1 copy-start.7
  260.6 213.7 %all-reduce.7.cloned.1.call-start = ((), (), s32[]{:S(2)}) async-start(), calls=%async_computation.5 | async-start | bytes 4718592 | tf_op jit(solution)/shard_map/psum | solution.py:64
  260.7 123.1 %copy-start.2 = (f32[64,1152]{1,0:T(8,128)S(1)}, f32[64,1152]{1,0:T(8,128)}, u32[]{:S(2)}) copy-start(f32[64,1152]{1,0:T(8,128)} %reduce-scatter.3.cloned.1.call-done) | copy-start | bytes 884740
  269.4 247.8 %all-gather.5.cloned.1.call-start = ((), (), s32[]{:S(2)}) async-start(), calls=%async_computation.7 | async-start | bytes 1327104 | tf_op jit(solution)/shard_map/all_gather | solution.py:68
  386.5 403.3 %all-reduce.9.cloned.1.call-start = ((), (), s32[]{:S(2)}) async-start(), calls=%async_computation.8 | async-start | bytes 2654208 | tf_op jit(solution)/shard_map/psum | solution.py:71
  474.3 2.4 copy-start.3
  476.7 40.5 %copy-start.4 = (bf16[512,144]{0,1:T(8,128)(2,1)S(1)}, bf16[512,144]{0,1:T(8,128)(2,1)}, u32[]{:S(2)}) copy-start(bf16[512,144]{0,1:T(8,128)(2,1)} %param.7) | copy-start | bytes 442372
Sparse Core Ops, SparseCore 0:
  11.2 44.7 reduce-scatter.2
  58.7 90.5 all-reduce.4
  152.6 92.6 all-gather.2
  260.7 122.9 reduce-scatter.4
  386.4 87.8 all-reduce.6
  476.7 40.4 all-gather.4
  520.7 269.0 all-reduce.8
where the time goes:
time: 801 us
  waiting for transfers between devices  721 us (90%)
  matrix products  31 us (4%)
  between operations  15.5 us (2%)
  blocking collectives  15 us (2%)
  other arithmetic  10.2 us (1%)
    psum x1, waiting for transfers between devices, on_device(): grad_image_head, grad_text_head = lax.psum((image_slice, text_slice), 'dp')  254 us
    reduce_scatter x1, waiting for transfers between devices, on_device(): lax.psum_scatter(text_terms.astype(jnp.bfloat16), 'dp', scatter_dimension...  114 us
    all_gather x1, waiting for transfers between devices, on_device(): piece = lax.all_gather(text_unit, 'dp', axis=0, tiled=True)  94.2 us
    psum x1, waiting for transfers between devices, on_device(): image_raw = lax.psum(image_part, 'tensor')  89 us
    psum x1, waiting for transfers between devices, on_device(): image_grad, loss_sum = lax.psum((image_grad, loss_sum), 'tensor')  87.7 us
    reduce_scatter x1, waiting for transfers between devices, on_device(): lax.psum_scatter(text_part, 'tensor', scatter_dimension=0, tiled=True)  42.8 us
    all_gather x1, waiting for transfers between devices, on_device(): group_back = lax.all_gather(text_back, 'tensor', axis=0, tiled=True)  38.8 us
  transfers between devices with their start and end apart: 7, of which 7 were waited for; matrix products, arithmetic and copies ran while one was open for 3% of the time, Pallas kernels for 0%

commit v1 on v0

v1 whole, which is shorter than its diff:
```python
import functools
import math

import jax
import jax.numpy as jnp
from jax import lax
from jax.experimental import pallas as pl
from jax.experimental.pallas import tpu as pltpu
from jax.sharding import Mesh, PartitionSpec as P

BF = jnp.bfloat16
F32 = jnp.float32
T = ("yl", "x")
PLANE = ("yh", "yl", "x")
SWAP = [(0, 1), (1, 0)]
LANE = 128
TILE = 256
LIMIT = 58 * 1024 * 1024


def spread(x, axes, n):
    wide = jnp.broadcast_to(x[None], (n,) + x.shape)
    return lax.all_to_all(wide, axes, 0, 0, tiled=True)


def contract(left, right, dims):
    return lax.dot_general(left, right, ((dims[:1], dims[1:]), ((), ())), preferred_element_type=F32)


def stats(raw):
    width = raw.shape[-1]
    mean_sq = jnp.mean(raw * raw, axis=-1, keepdims=True)
    return lax.rsqrt(mean_sq + 1e-06) * (1.0 / math.sqrt(width)), 1.0 / (width * (mean_sq + 1e-06))


def back(raw, grad):
    factor, inv = stats(raw)
    inner = jnp.sum(grad * raw, axis=-1, keepdims=True)
    return (factor * (grad - raw * (inner * inv))).astype(BF)


def head_copies(src, dst, sems, first):
    nt, nb = dst.shape[0], dst.shape[2] // LANE
    low = src.shape[1] if first is None else first
    out = []
    for b in range(nb):
        y, s = (0, b) if b < low else (1, b - nb + low)
        out.append(
            pltpu.make_async_copy(
                src.at[pl.ds(y * nt, nt), s], dst.at[:, :, pl.ds(b * LANE, LANE)], sems.at[b]
            )
        )
    return out


def split_rows(part, core, keep, give, head, t):
    half = part.shape[0] // 2
    low, high = part[:half], part[half:]
    first = core == 0
    keep[t, head] = jnp.where(first, low, high)
    give[t, head] = jnp.where(first, high, low).astype(BF)


def block_kernel(
    low, info, scalars, ids, packed, other, text_a, text_b,
    keep, give, loss,
    head_i, head_t, image, texts, raw_t, unit_t, unit_i, weight, backs, part, sems,
):
    nt, depth, width = head_i.shape
    full = nt * depth
    ni, nj = image.shape[2], texts.shape[0]
    core = info[0]
    scale, bias, coef = scalars[0], scalars[1], scalars[2]

    nb = width // LANE
    text_copies = [
        pltpu.make_async_copy(text_a, texts.at[pl.ds(0, nj // 2)], sems.at[2 * nb]),
        pltpu.make_async_copy(text_b, texts.at[pl.ds(nj // 2, nj // 2)], sems.at[2 * nb + 1]),
    ]
    half = ni // LANE // 2
    image_copies = [
        pltpu.make_async_copy(
            packed.at[pl.ds((b // half) * nt, nt), low + b % half],
            image.at[:, :, pl.ds(b * LANE, LANE)],
            sems.at[2 * nb + 2 + b],
        )
        for b in range(2 * half)
    ]
    sems_i, sems_t = sems.at[pl.ds(0, nb)], sems.at[pl.ds(nb, nb)]
    for copy in text_copies:
        copy.start()

    @pl.when(core == 0)
    def _():
        for copy in head_copies(other, head_t, sems_t, low):
            copy.start()
        for copy in head_copies(packed, head_i, sems_i, low):
            copy.start()

    @pl.when(core != 0)
    def _():
        for copy in head_copies(packed, head_t, sems_t, low):
            copy.start()
        for copy in head_copies(other, head_i, sems_i, low):
            copy.start()

    for copy in image_copies:
        copy.start()
    for copy in text_copies + head_copies(packed, head_t, sems_t, low):
        copy.wait()

    @pl.loop(0, nj // TILE)
    def _(j):
        here = pl.ds(pl.multiple_of(j * TILE, TILE), TILE)
        raw = contract(texts[here], head_t[...].reshape(full, width), (1, 0))
        raw_t[here] = raw
        unit_t[here] = (raw * stats(raw)[0]).astype(BF)

    for copy in head_copies(packed, head_i, sems_i, low) + image_copies:
        copy.wait()

    @pl.loop(0, ni // TILE)
    def _(i):
        here = pl.ds(pl.multiple_of(i * TILE, TILE), TILE)
        tile = image[:, :, here].reshape(full, TILE)
        raw = contract(tile, head_i[...].reshape(full, width), (0, 0))
        unit = (raw * stats(raw)[0]).astype(BF)
        unit_i[here] = unit
        scores = scale * contract(unit, unit_t[...], (1, 1)) + bias
        per = ni // 2 // TILE
        base = jnp.where(i < per, info[1], info[2]) + lax.rem(i, per) * TILE
        rows = base + lax.broadcasted_iota(jnp.int32, (TILE, 1), 0)
        match = rows == ids[...]
        small = jnp.exp(-jnp.abs(scores))
        soft = jnp.maximum(scores, 0.0) + jnp.log1p(small)
        sig = jnp.where(scores >= 0.0, 1.0, small) / (1.0 + small)
        terms = soft - jnp.where(match, scores, 0.0)
        total = terms[:, :LANE]
        for b in range(1, nj // LANE):
            total = total + terms[:, b * LANE : (b + 1) * LANE]
        loss[here] = total
        grads = jnp.where(match, sig - 1.0, sig).astype(BF)
        weight[here] = grads
        grad = coef * contract(grads, unit_t[...], (1, 0))
        backs[here] = back(raw, grad)

    @pl.loop(0, nt // 2)
    def _(k):
        rows = contract(image[pl.ds(2 * k, 2)].reshape(2 * depth, ni), backs[...], (1, 0))
        split_rows(rows[:depth], core, keep, give, 0, 2 * k)
        split_rows(rows[depth:], core, keep, give, 0, 2 * k + 1)

    for j in range(nj // TILE):
        here = pl.ds(j * TILE, TILE)
        grad = coef * contract(weight[:, here], unit_i[...], (0, 0))
        backs[here] = back(raw_t[here], grad)

    step = 3 * LANE
    for k in range(full // step):
        here = pl.ds(k * step, step)
        part[here] = contract(texts[:, here], backs[...], (0, 0))

    @pl.loop(0, nt)
    def _(k):
        rows = part[pl.ds(pl.multiple_of(k * depth, depth), depth)]
        split_rows(rows, core, keep, give, 1, k)


def on_device(image_feat, text_feat, image_head, text_head, logit_scale, logit_bias):
    nz, ny = lax.axis_size("z"), lax.axis_size("yh")
    nt = lax.axis_size("yl") * lax.axis_size("x")
    pairs, depth = image_feat.shape
    width = image_head.shape[1]
    half = depth // 2
    rows = pairs // nt
    full = nt * depth
    core = lax.axis_index("core")
    z = lax.axis_index("z")
    yh = lax.axis_index("yh")
    t = lax.axis_index(T)
    batch = pairs * nz * ny * 2
    coef = logit_scale[0] * (1.0 / math.sqrt(batch))

    nb = width // LANE
    low = -(-nb // 2)
    head = jnp.where(core == 0, image_head, text_head).reshape(depth, nb, LANE)
    head = jnp.where(yh == 0, head[:, :low], head[:, nb - low :]).transpose(1, 0, 2)
    columns = image_feat.T.reshape(depth, pairs // LANE, LANE).transpose(1, 0, 2)
    packed = lax.all_gather(jnp.concatenate([head, columns], axis=0), PLANE, axis=0)

    split = text_feat.reshape(nt, rows, depth)
    own = lax.all_to_all(split, T, 0, 0, tiled=True).transpose(1, 0, 2).reshape(rows, full)
    text_a = spread(own, "z", nz).reshape(nz * rows, full)
    text_b = lax.ppermute(text_a, "core", SWAP)
    packed, text_a, text_b = lax.optimization_barrier((packed, text_a, text_b))
    other = lax.ppermute(packed[:, :low], "core", SWAP)

    k = jnp.arange(nz * rows, dtype=jnp.int32)
    ids = jnp.concatenate(
        [((k // rows * ny + yh) * 2 + c) * pairs + t * rows + k % rows for c in (core, 1 - core)]
    )[None]
    info = jnp.stack([core] + [((z * ny + y) * 2 + core) * pairs for y in range(ny)])
    scalars = jnp.stack([logit_scale[0], logit_bias[0], coef])

    ni, nj = ny * pairs, 2 * nz * rows
    smem = pl.BlockSpec(memory_space=pltpu.SMEM)
    vmem = pl.BlockSpec(memory_space=pltpu.VMEM)
    hbm = pl.BlockSpec(memory_space=pl.ANY)
    keep, give, losses = pl.pallas_call(
        functools.partial(block_kernel, low),
        out_shape=[
            jax.ShapeDtypeStruct((nt, 2, half, width), F32),
            jax.ShapeDtypeStruct((nt, 2, half, width), BF),
            jax.ShapeDtypeStruct((ni, LANE), F32),
        ],
        in_specs=[smem, smem, vmem, hbm, hbm, hbm, hbm],
        out_specs=[vmem, vmem, vmem],
        scratch_shapes=[
            pltpu.VMEM((nt, depth, width), BF),
            pltpu.VMEM((nt, depth, width), BF),
            pltpu.VMEM((nt, depth, ni), BF),
            pltpu.VMEM((nj, full), BF),
            pltpu.VMEM((nj, width), F32),
            pltpu.VMEM((nj, width), BF),
            pltpu.VMEM((ni, width), BF),
            pltpu.VMEM((ni, nj), BF),
            pltpu.VMEM((max(ni, nj), width), BF),
            pltpu.VMEM((full, width), F32),
            pltpu.SemaphoreType.DMA((2 * nb + 2 + ni // LANE,)),
        ],
        compiler_params=pltpu.CompilerParams(vmem_limit_bytes=LIMIT),
        cost_estimate=pl.CostEstimate(
            flops=4 * (ni + nj) * full * width + 6 * ni * nj * width,
            bytes_accessed=20 * 1024 * 1024,
            transcendentals=3 * ni * nj,
        ),
        name="block",
    )(info, scalars, ids, packed, other, text_a, text_b)

    low_y = yh == 0
    losses = jnp.sum(losses, axis=1).reshape(ny, pairs)
    loss_mine = jnp.where(low_y, losses[0], losses[1])
    loss_give = jnp.where(low_y, losses[1], losses[0])
    loss = loss_mine + lax.ppermute(loss_give, "yh", SWAP)
    head_part = lax.reduce_precision(loss, 8, 7)
    row = jnp.concatenate([head_part, loss - head_part]).astype(BF)
    row = jnp.pad(row[None], ((0, 7), (0, width - 2 * pairs)))
    mine = (keep + lax.ppermute(give, "core", SWAP).astype(F32)).astype(BF)
    mine = mine.reshape(nt, 2 * half, width)
    mine = jnp.concatenate([mine, jnp.broadcast_to(row[None], (nt,) + row.shape)], axis=1)
    mine = lax.all_to_all(mine, T, 0, 0, tiled=True).astype(F32)
    row = jnp.sum(mine[:, 2 * half], axis=0)
    row_loss = (row[:pairs] + row[pairs : 2 * pairs]) / batch
    both = jnp.sum(mine[:, : 2 * half], axis=0).reshape(2, half, width)
    keep = jnp.where(low_y, both[0], both[1])
    give = jnp.where(low_y, both[1], both[0]).astype(BF)
    one = keep + lax.ppermute(give, "yh", SWAP).astype(F32)

    tiles = (half // 8) * nb
    per = -(-tiles // nz)
    one = one.astype(BF).reshape(half // 8, 8, nb, LANE).transpose(0, 2, 1, 3)
    one = jnp.pad(one.reshape(tiles, 8, LANE), ((0, per * nz - tiles), (0, 0), (0, 0)))
    one = lax.all_to_all(one.reshape(nz, per * 8, LANE), "z", 0, 0, tiled=True)
    one = jnp.sum(one.astype(F32), axis=0).astype(BF)
    one = spread(one, "z", nz).reshape(per * nz, 8, LANE)[:tiles]
    one = one.reshape(half // 8, nb, 8, LANE).transpose(0, 2, 1, 3).reshape(half, width)
    by_core = lax.ppermute(one, "core", SWAP)
    by_y = lax.ppermute(one, "yh", SWAP)
    by_both = lax.ppermute(one, ("yh", "core"), [(0, 3), (1, 2), (2, 1), (3, 0)])

    def join(mine, other):
        first = core == 0
        return jnp.concatenate([jnp.where(first, mine, other), jnp.where(first, other, mine)])

    here, there = join(one, by_core), join(by_y, by_both)
    out_i = jnp.where(low_y, here, there).astype(F32)
    out_t = jnp.where(low_y, there, here).astype(F32)
    return out_i, out_t, row_loss


def solution(mesh):
    fine = Mesh(mesh.devices.reshape(8, 2, 2, 2, 4), ("z", "yh", "core", "yl", "x"))
    dp = ("z", "yh", "core")
    placed = (P(dp, T), P(dp, T), P(T, None), P(T, None), P(), P())
    return jax.shard_map(
        on_device,
        mesh=fine,
        in_specs=placed,
        out_specs=(P(T, None), P(T, None), P(dp)),
        check_vma=False,
    )
```

time: 801 us -> 230 us (0.29)
  waiting for transfers between devices: 721 us -> 34.2 us
  blocking collectives: 15 us -> 99.8 us
  Pallas kernels: 0 us -> 36.5 us
  matrix products: 31 us -> 0 us
  starting transfers between devices: 0.29 us -> 23.2 us
    psum x3 -> x0, waiting for transfers between devices: 431 us -> none  [the longest x1 254 us: on_device(): grad_image_head, grad_text_head = lax.psum((image_slice, text_slice), 'dp')]
    reduce_scatter x2 -> x0, waiting for transfers between devices: 157 us -> none  [the longest x1 114 us: on_device(): lax.psum_scatter(text_terms.astype(jnp.bfloat16), 'dp', scatter_dimension...]
    all_gather x2 -> x1, waiting for transfers between devices: 133 us -> 9.19 us  [on_device(): lax.all_gather(jnp.concatenate([head, columns], axis=0), PLANE, axis=0)]
    all_to_all x0 -> x4, blocking collectives: none -> 99.8 us  [the longest x1 36.5 us: spread(): return lax.all_to_all(wide, axes, 0, 0, tiled=True)]
    pallas_call x0 -> x1, Pallas kernels: none -> 36.5 us  [on_device(): pl.pallas_call(functools.partial(block_kernel, low), out_shape=[jax.Shape...]
    dot_general x7 -> x0, matrix products: 31 us -> none  [the longest x3 9.57 us: contract_rows(): lax.dot_general(left, right, (((0,), (0,)), ((), ())), preferred_element_...]
    ppermute x0 -> x8, starting transfers between devices: none -> 19.8 us  [the longest x1 6.65 us: on_device(): by_core = lax.ppermute(one, 'core', SWAP)]
    ppermute x0 -> x8, waiting for transfers between devices: none -> 17.6 us  [the longest x1 4.18 us: on_device(): by_y = lax.ppermute(one, 'yh', SWAP)]
  transfers between devices with their start and end apart: 7 -> 10, of which waited for: 7 -> 8; matrix products, arithmetic and copies ran while one was open for 3% -> 2% of each run, Pallas kernels for 0% -> 0%
where the time goes in v1:
time: 230 us; the launch traced here: 229 us
  blocking collectives  99.8 us (43%)
  Pallas kernels  36.5 us (16%)
  waiting for transfers between devices  34.2 us (15%)
  starting transfers between devices  23.2 us (10%)
  between operations  15.5 us (7%)
  other arithmetic  11.3 us (5%)
  local copies, waits for them, and re-layouts  8.58 us (4%)
    all_to_all x1, blocking collectives, spread(): return lax.all_to_all(wide, axes, 0, 0, tiled=True)  36.5 us
    pallas_call x1, Pallas kernels, on_device(): pl.pallas_call(functools.partial(block_kernel, low), out_shape=[jax.Shape...  36.5 us
    all_to_all x1, blocking collectives, on_device(): mine = lax.all_to_all(mine, T, 0, 0, tiled=True).astype(F32)  36.4 us
    all_to_all x1, blocking collectives, on_device(): one = lax.all_to_all(one.reshape(nz, per * 8, LANE), 'z', 0, 0, tiled=True)  15 us
    all_to_all x1, blocking collectives, on_device(): lax.all_to_all(split, T, 0, 0, tiled=True).transpose(1, 0, 2)  11.9 us
    all_gather x1, waiting for transfers between devices, on_device(): lax.all_gather(jnp.concatenate([head, columns], axis=0), PLANE, axis=0)  9.19 us
    all_to_all x1, waiting for transfers between devices, spread(): return lax.all_to_all(wide, axes, 0, 0, tiled=True)  7.37 us
    ppermute x1, starting transfers between devices, on_device(): by_core = lax.ppermute(one, 'core', SWAP)  6.65 us
  transfers between devices with their start and end apart: 10, of which 8 were waited for; matrix products, arithmetic and copies ran while one was open for 2% of the time, Pallas kernels for 0%

profile of v1, /device:TPU:1, one launch (start us, length us, event | category | flops | bytes accessed | tf_op | source)
XLA Modules:
  0.0 229.2 jit_solution(9017150332117652574)
XLA Ops:
  7.2 0.9 reshape.87
  8.2 1.0 broadcast_select_fusion
  9.2 0.2 reshape.86
  9.4 0.1 fusion
  9.5 0.2 pad_maximum_fusion.1
  9.8 0.8 copy.17
  10.6 0.1 copy.20
  10.7 11.9 %all_to_all.25 = bf16[8,64,144]{2,1,0:T(8,128)(2,1)S(1)} all-to-all(bf16[8,64,144]{2,1,0:T(8,128)(2,1)S(1)} %bitcast.31), channel_id=1, replica_groups=mesh['z'=8,'yh'=2,'core'=2,'yl'=2,'x'=4] {'yl','x'}, dimensions={0} | all-to-all | bytes 294912 | tf_op jit(solution)/shard_map/all_to_all | solution.py:192
  22.7 0.1 copy.19
  22.8 0.3 broadcast_in_dim.11
  23.1 0.1 broadcast_in_dim.12
  23.3 36.5 %all_to_all.26 = bf16[8,64,1152]{2,1,0:T(8,128)(2,1)S(1)} all-to-all(bf16[8,64,1152]{2,1,0:T(8,128)(2,1)S(1)} %broadcast_in_dim.12), channel_id=1, replica_groups=mesh['z'=8,'yh'=2,'core'=2,'yl'=2,'x'=4] {'z'}, dimensions={0} | all-to-all | bytes 2359296 | tf_op jit(solution)/shard_map/all_to_all | solution.py:23
  59.8 1.0 copy-done.1
  60.8 4.0 %collective-permute-start = (bf16[512,1152]{1,0:T(8,128)(2,1)S(1)}, bf16[512,1152]{1,0:T(8,128)(2,1)}, u32[]{:S(2)}, u32[]{:S(2)}) collective-permute-start(bf16[512,1152]{1,0:T(8,128)(2,1)S(1)} %bitcast.28), channel_id=1, source_target_pairs={{0,8},{8,0},{1,9},{9,1},{2,10},{10,2},{3,11},{11,3},{4,12},{12,4},... | collective-permute-start | bytes 3538952 | tf_op jit(solution)/shard_map/ppermute | solution.py:194
  64.8 2.6 %collective-permute-done.text_b = bf16[512,1152]{1,0:T(8,128)(2,1)} collective-permute-done((bf16[512,1152]{1,0:T(8,128)(2,1)S(1)}, bf16[512,1152]{1,0:T(8,128)(2,1)}, u32[]{:S(2)}, u32[]{:S(2)}) %collective-permute-start) | collective-permute-done | bytes 1179680 | tf_op jit(solution)/shard_map/ppermute | solution.py:194
  67.4 9.2 %all-gather.3.cloned.1.call-done = bf16[144,144,128]{2,1,0:T(8,128)(2,1)} async-done(((bf16[9,144,128]{2,1,0:T(8,128)(2,1)}), bf16[144,144,128]{2,1,0:T(8,128)(2,1)}) %all-gather.3.cloned.1.call-update) | async-done | bytes 5308432 | tf_op jit(solution)/shard_map/all_gather | solution.py:189
  76.6 2.0 slice.46
  78.6 0.8 collective-permute-start.1
  80.6 0.7 pad_maximum_fusion.4.scalars
  81.3 0.6 pad_add_fusion.1.info
  81.9 0.6 pad_add_fusion
  82.5 2.0 collective-permute-done.1.other
  84.5 36.5 %block.1 = (f32[8,2,72,1152]{3,2,1,0:T(8,128)}, bf16[8,2,72,1152]{3,2,1,0:T(8,128)(2,1)}, f32[1024,128]{1,0:T(8,128)}) custom-call(s32[3]{0:T(128)} %pad_add_fusion.1.info, f32[3]{0:T(128)} %pad_maximum_fusion.4.scalars, s32[1,1024]{1,0:T(1,128)} %bitcast.41, bf16[16,9,144,128]{3,2,1,0:T(8,128)(2,1)} %bitcast.27, ...), custom_call_target="tpu_custom_call" | custom-call | flops 18119393280 | bytes 20971520 | tf_op jit(solution)/shard_map/block/pallas_call | solution.py:209
  121.0 0.5 collective-permute-start.2
  121.5 1.2 reduce_sum.39
  122.7 3.0 %collective-permute-start.3 = (f32[512]{0:T(512)S(1)}, f32[512]{0:T(512)S(1)}, u32[]{:S(2)}, u32[]{:S(2)}) collective-permute-start(f32[512]{0:T(512)S(1)} %slice_select_fusion.1), channel_id=1, source_target_pairs={{0,16},{16,0},{1,17},{17,1},{2,18},{18,2},{3,19},{19,3},{4,20},{20... | collective-permute-start | bytes 6152 | tf_op jit(solution)/shard_map/ppermute | solution.py:244
  125.7 1.3 collective-permute-done.3
  127.0 3.0 %add_convert_fusion = bf16[8,2,72,1152]{3,2,1,0:T(8,128)(2,1)S(1)} fusion(f32[8,2,72,1152]{3,2,1,0:T(8,128)} %get-tuple-element.12, bf16[8,2,72,1152]{3,2,1,0:T(8,128)(2,1)S(1)} %collective-permute-done.2), kind=kLoop, calls=%fused_computation.1 | loop fusion | flops 3981312 | bytes 10616832 | tf_op jit(solution)/shard_map/convert_element_type | solution.py:248
  130.1 0.2 pad_maximum_fusion
  130.3 36.4 %all_to_all.27 = bf16[8,152,1152]{2,1,0:T(8,128)(2,1)S(1)} all-to-all(bf16[8,152,1152]{2,1,0:T(8,128)(2,1)S(1)} %pad_maximum_fusion), channel_id=1, replica_groups=mesh['z'=8,'yh'=2,'core'=2,'yl'=2,'x'=4] {'yl','x'}, dimensions={0} | all-to-all | bytes 5603328 | tf_op jit(solution)/shard_map/all_to_all | solution.py:251
  166.7 0.4 convert_element_type.40
  167.1 0.3 slice_reduce_fusion
  167.3 2.2 copy-done
  169.5 1.9 collective-permute-start.4
  171.4 3.9 %collective-permute-done.4 = bf16[72,1152]{1,0:T(8,128)(2,1)S(1)} collective-permute-done((bf16[72,1152]{1,0:T(8,128)(2,1)S(1)}, bf16[72,1152]{1,0:T(8,128)(2,1)S(1)}, u32[]{:S(2)}, u32[]{:S(2)}) %collective-permute-start.4) | collective-permute-done | bytes 165920 | tf_op jit(solution)/shard_map/ppermute | solution.py:257
  175.3 0.1 add_convert_fusion.1
  175.4 15.0 %all_to_all.28 = bf16[8,88,128]{2,1,0:T(8,128)(2,1)S(1)} all-to-all(bf16[8,88,128]{2,1,0:T(8,128)(2,1)S(1)} %bitcast.32), channel_id=1, replica_groups=mesh['z'=8,'yh'=2,'core'=2,'yl'=2,'x'=4] {'z'}, dimensions={0} | all-to-all | bytes 360448 | tf_op jit(solution)/shard_map/all_to_all | solution.py:263
  190.4 0.7 broadcast_in_dim.27
  191.1 3.4 %all-to-all-start.4 = ((bf16[8,88,128]{2,1,0:T(8,128)(2,1)}), bf16[8,88,128]{2,1,0:T(8,128)(2,1)S(1)}, u32[]{:S(2)}, u32[]{:S(2)}) async-start(bf16[8,88,128]{2,1,0:T(8,128)(2,1)} %broadcast_in_dim.27), calls=%async_computation.4 | async-start | bytes 360448 | tf_op jit(solution)/shard_map/all_to_all | solution.py:23
  194.5 1.0 slice_reduce_fusion.1
  195.5 7.4 %all-to-all-done.4 = bf16[8,88,128]{2,1,0:T(8,128)(2,1)S(1)} async-done(((bf16[8,88,128]{2,1,0:T(8,128)(2,1)}), bf16[8,88,128]{2,1,0:T(8,128)(2,1)S(1)}, u32[]{:S(2)}, u32[]{:S(2)}) %all-to-all-start.4) | async-done | bytes 180256 | tf_op jit(solution)/shard_map/all_to_all | solution.py:23
  202.9 6.7 %collective-permute-start.5 = (bf16[72,1152]{1,0:T(8,128)(2,1)S(1)}, bf16[72,1152]{1,0:T(8,128)(2,1)S(1)}, u32[]{:S(2)}, u32[]{:S(2)}) collective-permute-start(bf16[72,1152]{1,0:T(8,128)(2,1)S(1)} %bitcast.35), channel_id=1, source_target_pairs={{0,8},{8,0},{1,9},{9,1},{2,10},{10,2},{3,11},{11,3},{4,12},{12,4},... | collective-permute-start | bytes 497672 | tf_op jit(solution)/shard_map/ppermute | solution.py:267
  209.5 0.6 fusion.16
  210.1 1.8 collective-permute-start.6
  211.9 1.4 collective-permute-start.7
  213.3 4.2 %collective-permute-done.6 = bf16[72,1152]{1,0:T(8,128)(2,1)S(1)} collective-permute-done((bf16[72,1152]{1,0:T(8,128)(2,1)S(1)}, bf16[72,1152]{1,0:T(8,128)(2,1)S(1)}, u32[]{:S(2)}, u32[]{:S(2)}) %collective-permute-start.6) | collective-permute-done | bytes 165920 | tf_op jit(solution)/shard_map/ppermute | solution.py:268
  217.5 3.7 %collective-permute-done.7 = bf16[72,1152]{1,0:T(8,128)(2,1)S(1)} collective-permute-done((bf16[72,1152]{1,0:T(8,128)(2,1)S(1)}, bf16[72,1152]{1,0:T(8,128)(2,1)S(1)}, u32[]{:S(2)}, u32[]{:S(2)}) %collective-permute-start.7) | collective-permute-done | bytes 165920 | tf_op jit(solution)/shard_map/ppermute | solution.py:269
  221.2 1.1 select_convert_fusion
  (22 shorter events, 0.3 us)
Async XLA Ops:
  7.2 3.4 %copy-start.2 = (bf16[512,144]{0,1:T(8,128)(2,1)S(1)}, bf16[512,144]{0,1:T(8,128)(2,1)}, u32[]{:S(2)}) copy-start(bf16[512,144]{0,1:T(8,128)(2,1)} %param.7) | copy-start | bytes 442372
  7.2 69.4 %all-gather.3.cloned.1.call-start = ((), (), s32[]{:S(2)}) async-start(), calls=%async_computation.5 | async-start | bytes 5640192 | tf_op jit(solution)/shard_map/all_gather | solution.py:189
  59.8 1.0 copy-start.1
  60.8 6.6 %collective-permute-start = (bf16[512,1152]{1,0:T(8,128)(2,1)S(1)}, bf16[512,1152]{1,0:T(8,128)(2,1)}, u32[]{:S(2)}, u32[]{:S(2)}) collective-permute-start(bf16[512,1152]{1,0:T(8,128)(2,1)S(1)} %bitcast.28), channel_id=1, source_target_pairs={{0,8},{8,0},{1,9},{9,1},{2,10},{10,2},{3,11},{11,3},{4,12},{12,4},... | collective-permute-start | bytes 3538952 | tf_op jit(solution)/shard_map/ppermute | solution.py:194
  78.6 5.9 %collective-permute-start.1 = (bf16[16,5,144,128]{3,2,1,0:T(8,128)(2,1)S(1)}, bf16[16,5,144,128]{3,2,1,0:T(8,128)(2,1)}, u32[]{:S(2)}, u32[]{:S(2)}) collective-permute-start(bf16[16,5,144,128]{3,2,1,0:T(8,128)(2,1)S(1)} %slice.46), channel_id=1, source_target_pairs={{0,8},{8,0},{1,9},{9,1},{2,10},{10,2},{3,11},{11,3},{4,12},{12,4},... | collective-permute-start | bytes 8847368 | tf_op jit(solution)/shard_map/ppermute | solution.py:196
  121.0 6.0 %collective-permute-start.2 = (bf16[8,2,72,1152]{3,2,1,0:T(8,128)(2,1)}, bf16[8,2,72,1152]{3,2,1,0:T(8,128)(2,1)S(1)}, u32[]{:S(2)}, u32[]{:S(2)}) collective-permute-start(bf16[8,2,72,1152]{3,2,1,0:T(8,128)(2,1)} %get-tuple-element.13), channel_id=1, source_target_pairs={{0,8},{8,0},{1,9},{9,1},{2,10},{10,2},{3,11},{11,3},{4,12},{12,4},... | collective-permute-start | bytes 7962632 | tf_op jit(solution)/shard_map/ppermute | solution.py:248
  122.7 4.2 %collective-permute-start.3 = (f32[512]{0:T(512)S(1)}, f32[512]{0:T(512)S(1)}, u32[]{:S(2)}, u32[]{:S(2)}) collective-permute-start(f32[512]{0:T(512)S(1)} %slice_select_fusion.1), channel_id=1, source_target_pairs={{0,16},{16,0},{1,17},{17,1},{2,18},{18,2},{3,19},{19,3},{4,20},{20... | collective-permute-start | bytes 6152 | tf_op jit(solution)/shard_map/ppermute | solution.py:244
  167.1 2.4 %copy-start = (f32[8,152,1152]{2,1,0:T(8,128)}, f32[8,152,1152]{2,1,0:T(8,128)S(1)}, u32[]{:S(2)}) copy-start(f32[8,152,1152]{2,1,0:T(8,128)S(1)} %convert_element_type.40) | copy-start | bytes 16809988
  169.5 5.8 %collective-permute-start.4 = (bf16[72,1152]{1,0:T(8,128)(2,1)S(1)}, bf16[72,1152]{1,0:T(8,128)(2,1)S(1)}, u32[]{:S(2)}, u32[]{:S(2)}) collective-permute-start(bf16[72,1152]{1,0:T(8,128)(2,1)S(1)} %select_convert_fusion.2), channel_id=1, source_target_pairs={{0,16},{16,0},{1,17},{17,1},{2,18},{18,2},{3,19},{19,3},{4,20},{20... | collective-permute-start | bytes 497672 | tf_op jit(solution)/shard_map/ppermute | solution.py:257
  191.1 11.8 %all-to-all-start.4 = ((bf16[8,88,128]{2,1,0:T(8,128)(2,1)}), bf16[8,88,128]{2,1,0:T(8,128)(2,1)S(1)}, u32[]{:S(2)}, u32[]{:S(2)}) async-start(bf16[8,88,128]{2,1,0:T(8,128)(2,1)} %broadcast_in_dim.27), calls=%async_computation.4 | async-start | bytes 360448 | tf_op jit(solution)/shard_map/all_to_all | solution.py:23
  202.9 10.4 %collective-permute-start.5 = (bf16[72,1152]{1,0:T(8,128)(2,1)S(1)}, bf16[72,1152]{1,0:T(8,128)(2,1)S(1)}, u32[]{:S(2)}, u32[]{:S(2)}) collective-permute-start(bf16[72,1152]{1,0:T(8,128)(2,1)S(1)} %bitcast.35), channel_id=1, source_target_pairs={{0,8},{8,0},{1,9},{9,1},{2,10},{10,2},{3,11},{11,3},{4,12},{12,4},... | collective-permute-start | bytes 497672 | tf_op jit(solution)/shard_map/ppermute | solution.py:267
  210.1 7.4 %collective-permute-start.6 = (bf16[72,1152]{1,0:T(8,128)(2,1)S(1)}, bf16[72,1152]{1,0:T(8,128)(2,1)S(1)}, u32[]{:S(2)}, u32[]{:S(2)}) collective-permute-start(bf16[72,1152]{1,0:T(8,128)(2,1)S(1)} %bitcast.36), channel_id=1, source_target_pairs={{0,16},{16,0},{1,17},{17,1},{2,18},{18,2},{3,19},{19,3},{4,20},{20... | collective-permute-start | bytes 497672 | tf_op jit(solution)/shard_map/ppermute | solution.py:268
  211.9 9.2 %collective-permute-start.7 = (bf16[72,1152]{1,0:T(8,128)(2,1)S(1)}, bf16[72,1152]{1,0:T(8,128)(2,1)S(1)}, u32[]{:S(2)}, u32[]{:S(2)}) collective-permute-start(bf16[72,1152]{1,0:T(8,128)(2,1)S(1)} %bitcast.37), channel_id=1, source_target_pairs={{0,24},{8,16},{16,8},{24,0},{1,25},{9,17},{17,9},{25,1},{2,26},{10... | collective-permute-start | bytes 497672 | tf_op jit(solution)/shard_map/ppermute | solution.py:269
Sparse Core Ops, SparseCore 0:
  11.0 65.4 all-gather.2

commit v2 on v1

v2 whole, which is shorter than its diff:
```python
import functools
import math

import jax
import jax.numpy as jnp
from jax import lax
from jax.experimental import pallas as pl
from jax.experimental.pallas import tpu as pltpu
from jax.sharding import Mesh, PartitionSpec as P

BF = jnp.bfloat16
F32 = jnp.float32
T = ("yl", "x")
PLANE = ("yh", "yl", "x")
ZY = ("z", "yh")
SWAP = [(0, 1), (1, 0)]
LANE = 128
TILE = 512
LIMIT = 58 * 1024 * 1024


def spread(x, axes, n):
    wide = jnp.broadcast_to(x[None], (n,) + x.shape)
    return lax.all_to_all(wide, axes, 0, 0, tiled=True)


def contract(left, right, dims):
    return lax.dot_general(left, right, ((dims[:1], dims[1:]), ((), ())), preferred_element_type=F32)


def stats(raw):
    width = raw.shape[-1]
    mean_sq = jnp.mean(raw * raw, axis=-1, keepdims=True)
    return lax.rsqrt(mean_sq + 1e-06) * (1.0 / math.sqrt(width)), 1.0 / (width * (mean_sq + 1e-06))


def back(raw, grad):
    factor, inv = stats(raw)
    inner = jnp.sum(grad * raw, axis=-1, keepdims=True)
    return (factor * (grad - raw * (inner * inv))).astype(BF)


def head_copies(src, dst, sems, first):
    nt, nb = dst.shape[0], dst.shape[2] // LANE
    low = src.shape[1] if first is None else first
    out = []
    for b in range(nb):
        y, s = (0, b) if b < low else (1, b - nb + low)
        out.append(
            pltpu.make_async_copy(
                src.at[pl.ds(y * nt, nt), s], dst.at[:, :, pl.ds(b * LANE, LANE)], sems.at[b]
            )
        )
    return out


def block_kernel(
    low, info, scalars, ids, packed, other, text_a, text_b,
    keep, give, loss,
    head_i, head_t, image, texts, raw_t, unit_t, unit_i, weight, backs, part_i, part_t, sems, out_sems,
):
    nt, depth, width = head_i.shape
    full = nt * depth
    ni, nj = image.shape[2], texts.shape[0]
    core = info[0]
    scale, bias, coef = scalars[0], scalars[1], scalars[2]

    nb = width // LANE
    text_copies = [
        pltpu.make_async_copy(text_a, texts.at[pl.ds(0, nj // 2)], sems.at[2 * nb]),
        pltpu.make_async_copy(text_b, texts.at[pl.ds(nj // 2, nj // 2)], sems.at[2 * nb + 1]),
    ]
    half = ni // LANE // 2
    image_copies = [
        pltpu.make_async_copy(
            packed.at[pl.ds((b // half) * nt, nt), low + b % half],
            image.at[:, :, pl.ds(b * LANE, LANE)],
            sems.at[2 * nb + 2 + b],
        )
        for b in range(2 * half)
    ]
    sems_i, sems_t = sems.at[pl.ds(0, nb)], sems.at[pl.ds(nb, nb)]

    def start_head(dst, at, mine):
        @pl.when(core == mine)
        def _():
            for copy in head_copies(packed, dst, at, low):
                copy.start()

        @pl.when(core != mine)
        def _():
            for copy in head_copies(other, dst, at, low):
                copy.start()

    for copy in text_copies:
        copy.start()
    start_head(head_t, sems_t, 1)
    for copy in text_copies + head_copies(packed, head_t, sems_t, low):
        copy.wait()
    start_head(head_i, sems_i, 0)
    for copy in image_copies:
        copy.start()

    @pl.loop(0, nj // TILE)
    def _(j):
        here = pl.ds(pl.multiple_of(j * TILE, TILE), TILE)
        raw = contract(texts[here], head_t[...].reshape(full, width), (1, 0))
        raw_t[here] = raw
        unit_t[here] = (raw * stats(raw)[0]).astype(BF)

    for copy in head_copies(packed, head_i, sems_i, low) + image_copies:
        copy.wait()

    for i in range(ni // TILE):
        here = pl.ds(i * TILE, TILE)
        tile = image[:, :, here].reshape(full, TILE)
        raw = contract(tile, head_i[...].reshape(full, width), (0, 0))
        unit = (raw * stats(raw)[0]).astype(BF)
        unit_i[here] = unit
        scores = scale * contract(unit, unit_t[...], (1, 1)) + bias
        per = ni // 2 // TILE
        base = info[1 + i // per] + i % per * TILE
        rows = base + lax.broadcasted_iota(jnp.int32, (TILE, 1), 0)
        match = rows == ids[...]
        small = jnp.exp(-jnp.abs(scores))
        soft = jnp.maximum(scores, 0.0) + jnp.log1p(small)
        sig = jnp.where(scores >= 0.0, 1.0, small) / (1.0 + small)
        terms = soft - jnp.where(match, scores, 0.0)
        total = terms[:, :LANE]
        for b in range(1, nj // LANE):
            total = total + terms[:, b * LANE : (b + 1) * LANE]
        loss[:, here] = jnp.sum(total.T, axis=0, keepdims=True)
        grads = jnp.where(match, sig - 1.0, sig).astype(BF)
        weight[here] = grads
        grad = coef * contract(grads, unit_t[...], (1, 0))
        backs[here] = back(raw, grad)

    step = 3 * LANE

    def out_copy(src, dst, at, k):
        here = pl.ds(k * step, step)
        return pltpu.make_async_copy(src.at[here], dst.at[here], out_sems.at[at + k])

    def send(src, at, mine, k):
        @pl.when(core == mine)
        def _():
            out_copy(src, keep, at, k).start()

        @pl.when(core != mine)
        def _():
            out_copy(src, give, at, k).start()

    wide = nt // 2 * depth
    for k in range(2):
        rows = image[pl.ds(k * nt // 2, nt // 2)].reshape(wide, ni)
        part_i[pl.ds(k * wide, wide)] = contract(rows, backs[...], (1, 0)).astype(BF)
    for k in range(full // step):
        send(part_i, 0, 0, k)

    for j in range(nj // TILE):
        here = pl.ds(j * TILE, TILE)
        grad = coef * contract(weight[:, here], unit_i[...], (0, 0))
        backs[here] = back(raw_t[here], grad)

    for k in range(full // step):
        here = pl.ds(k * step, step)
        part_t[here] = contract(texts[:, here], backs[...], (0, 0)).astype(BF)
        send(part_t, full // step, 1, k)

    for k in range(full // step):
        out_copy(part_i, keep, 0, k).wait()
        out_copy(part_t, give, full // step, k).wait()


def on_device(image_feat, text_feat, image_head, text_head, logit_scale, logit_bias):
    nz, ny = lax.axis_size("z"), lax.axis_size("yh")
    nt = lax.axis_size("yl") * lax.axis_size("x")
    pairs, depth = image_feat.shape
    width = image_head.shape[1]
    rows = pairs // nt
    full = nt * depth
    core = lax.axis_index("core")
    z = lax.axis_index("z")
    yh = lax.axis_index("yh")
    t = lax.axis_index(T)
    batch = pairs * nz * ny * 2
    coef = logit_scale[0] * (1.0 / math.sqrt(batch))

    nb = width // LANE
    low = -(-nb // 2)
    head = jnp.where(core == 0, image_head, text_head).reshape(depth, nb, LANE)
    head = jnp.where(yh == 0, head[:, :low], head[:, nb - low :]).transpose(1, 0, 2)
    columns = image_feat.T.reshape(depth, pairs // LANE, LANE).transpose(1, 0, 2)
    packed = lax.all_gather(jnp.concatenate([head, columns], axis=0), PLANE, axis=0)

    split = text_feat.reshape(nt, rows, depth)
    own = lax.all_to_all(split, T, 0, 0, tiled=True).transpose(1, 0, 2).reshape(rows, full)
    text_a = spread(own, "z", nz).reshape(nz * rows, full)
    text_b = lax.ppermute(text_a, "core", SWAP)
    k = jnp.arange(nz * rows, dtype=jnp.int32)
    ids = jnp.concatenate(
        [((k // rows * ny + yh) * 2 + c) * pairs + t * rows + k % rows for c in (core, 1 - core)]
    )[None]
    info = jnp.stack([core] + [((z * ny + y) * 2 + core) * pairs for y in range(ny)])
    scalars = jnp.stack([logit_scale[0], logit_bias[0], coef])

    packed, text_a, text_b, ids, info, scalars = lax.optimization_barrier(
        (packed, text_a, text_b, ids, info, scalars)
    )
    other = lax.ppermute(packed[:, :low], "core", SWAP)

    ni, nj = ny * pairs, 2 * nz * rows
    smem = pl.BlockSpec(memory_space=pltpu.SMEM)
    vmem = pl.BlockSpec(memory_space=pltpu.VMEM)
    hbm = pl.BlockSpec(memory_space=pl.ANY)
    keep, give, losses = pl.pallas_call(
        functools.partial(block_kernel, low),
        out_shape=[
            jax.ShapeDtypeStruct((full, width), BF),
            jax.ShapeDtypeStruct((full, width), BF),
            jax.ShapeDtypeStruct((1, ni), F32),
        ],
        in_specs=[smem, smem, vmem, hbm, hbm, hbm, hbm],
        out_specs=[hbm, hbm, vmem],
        scratch_shapes=[
            pltpu.VMEM((nt, depth, width), BF),
            pltpu.VMEM((nt, depth, width), BF),
            pltpu.VMEM((nt, depth, ni), BF),
            pltpu.VMEM((nj, full), BF),
            pltpu.VMEM((nj, width), F32),
            pltpu.VMEM((nj, width), BF),
            pltpu.VMEM((ni, width), BF),
            pltpu.VMEM((ni, nj), BF),
            pltpu.VMEM((max(ni, nj), width), BF),
            pltpu.VMEM((full, width), BF),
            pltpu.VMEM((full, width), BF),
            pltpu.SemaphoreType.DMA((2 * nb + 2 + ni // LANE,)),
            pltpu.SemaphoreType.DMA((2 * (full // (3 * LANE)),)),
        ],
        compiler_params=pltpu.CompilerParams(vmem_limit_bytes=LIMIT),
        cost_estimate=pl.CostEstimate(
            flops=4 * (ni + nj) * full * width + 6 * ni * nj * width,
            bytes_accessed=20 * 1024 * 1024,
            transcendentals=3 * ni * nj,
        ),
        name="block",
    )(info, scalars, ids, packed, other, text_a, text_b)

    low_y = yh == 0
    losses = losses.reshape(ny, pairs)
    loss_mine = jnp.where(low_y, losses[0], losses[1])
    loss_give = jnp.where(low_y, losses[1], losses[0])
    loss = loss_mine + lax.ppermute(loss_give, "yh", SWAP)
    head_part = lax.reduce_precision(loss, 8, 7)
    row = jnp.concatenate([head_part, loss - head_part]).astype(BF)
    row = jnp.pad(row[None], ((0, 7), (0, width - 2 * pairs)))
    mine = (keep.astype(F32) + lax.ppermute(give, "core", SWAP).astype(F32)).astype(BF)
    mine = mine.reshape(nt, depth, width)
    mine = jnp.concatenate([mine, jnp.broadcast_to(row[None], (nt,) + row.shape)], axis=1)
    mine = lax.all_to_all(mine, T, 0, 0, tiled=True).astype(F32)
    row = jnp.sum(mine[:, depth], axis=0)
    row_loss = (row[:pairs] + row[pairs : 2 * pairs]) / batch
    one = jnp.sum(mine[:, :depth], axis=0).astype(BF)

    n = nz * ny
    tiles = (depth // 8) * nb
    per = -(-tiles // n)
    one = one.reshape(depth // 8, 8, nb, LANE).transpose(0, 2, 1, 3)
    one = jnp.pad(one.reshape(tiles, 8, LANE), ((0, per * n - tiles), (0, 0), (0, 0)))
    one = lax.all_to_all(one.reshape(n, per * 8, LANE), ZY, 0, 0, tiled=True)
    one = jnp.sum(one.astype(F32), axis=0).astype(BF)
    one = spread(one, ZY, n).reshape(per * n, 8, LANE)[:tiles]
    one = one.reshape(depth // 8, nb, 8, LANE).transpose(0, 2, 1, 3).reshape(depth, width)
    two = lax.ppermute(one, "core", SWAP)
    out_i = jnp.where(core == 0, one, two).astype(F32)
    out_t = jnp.where(core == 0, two, one).astype(F32)
    return out_i, out_t, row_loss


def solution(mesh):
    fine = Mesh(mesh.devices.reshape(8, 2, 2, 2, 4), ("z", "yh", "core", "yl", "x"))
    dp = ("z", "yh", "core")
    placed = (P(dp, T), P(dp, T), P(T, None), P(T, None), P(), P())
    return jax.shard_map(
        on_device,
        mesh=fine,
        in_specs=placed,
        out_specs=(P(T, None), P(T, None), P(dp)),
        check_vma=False,
    )
```

time: 230 us -> 213 us (0.926)
  blocking collectives: 99.8 us -> 121 us
  waiting for transfers between devices: 34.2 us -> 16.1 us
  starting transfers between devices: 23.2 us -> 12.5 us
  Pallas kernels: 36.5 us -> 30.2 us
    all_to_all x1 -> x2, blocking collectives: 36.5 us -> 52.3 us  [spread(): return lax.all_to_all(wide, axes, 0, 0, tiled=True)]
    ppermute x5 -> x2, waiting for transfers between devices: 11.8 us -> 0.09 us  [the longest x1 0.09 us: on_device(): lax.ppermute(give, 'core', SWAP).astype(F32)]
    all_to_all x1 -> x0, waiting for transfers between devices: 7.37 us -> none  [spread(): return lax.all_to_all(wide, axes, 0, 0, tiled=True)]
    ppermute x5 -> x2, starting transfers between devices: 12.1 us -> 5.07 us  [the longest x1 4.56 us: on_device(): two = lax.ppermute(one, 'core', SWAP)]
    pallas_call x1, Pallas kernels: 36.5 us -> 30.2 us  [on_device(): pl.pallas_call(functools.partial(block_kernel, low), out_shape=[jax.Shape...]
    all_to_all x1, blocking collectives: 15 us -> 20.3 us  [on_device(): one = lax.all_to_all(one.reshape(n, per * 8, LANE), ZY, 0, 0, tiled=True)]
    all_to_all x1 -> x0, starting transfers between devices: 3.39 us -> none  [spread(): return lax.all_to_all(wide, axes, 0, 0, tiled=True)]
    ppermute x1, waiting for transfers between devices: 1.96 us -> 5.14 us  [on_device(): other = lax.ppermute(packed[:, :low], 'core', SWAP)]
  transfers between devices with their start and end apart: 10 -> 6, of which waited for: 8 -> 4; matrix products, arithmetic and copies ran while one was open for 2% -> 2% of each run, Pallas kernels for 0% -> 0%
where the time goes in v2:
time: 213 us; the launch traced here: 212 us
  blocking collectives  121 us (57%)
  Pallas kernels  30.2 us (14%)
  waiting for transfers between devices  16.1 us (8%)
  between operations  15.5 us (7%)
  starting transfers between devices  12.5 us (6%)
  other arithmetic  10.1 us (5%)
  local copies, waits for them, and re-layouts  6.96 us (3%)
    all_to_all x2, blocking collectives, spread(): return lax.all_to_all(wide, axes, 0, 0, tiled=True)  52.3 us
    all_to_all x1, blocking collectives, on_device(): mine = lax.all_to_all(mine, T, 0, 0, tiled=True).astype(F32)  36.5 us
    pallas_call x1, Pallas kernels, on_device(): pl.pallas_call(functools.partial(block_kernel, low), out_shape=[jax.Shape...  30.2 us
    all_to_all x1, blocking collectives, on_device(): one = lax.all_to_all(one.reshape(n, per * 8, LANE), ZY, 0, 0, tiled=True)  20.3 us
    all_to_all x1, blocking collectives, on_device(): lax.all_to_all(split, T, 0, 0, tiled=True).transpose(1, 0, 2)  11.9 us
    all_gather x1, waiting for transfers between devices, on_device(): lax.all_gather(jnp.concatenate([head, columns], axis=0), PLANE, axis=0)  9.61 us
    ppermute x1, waiting for transfers between devices, on_device(): other = lax.ppermute(packed[:, :low], 'core', SWAP)  5.14 us
    ppermute x1, starting transfers between devices, on_device(): two = lax.ppermute(one, 'core', SWAP)  4.56 us
  transfers between devices with their start and end apart: 6, of which 4 were waited for; matrix products, arithmetic and copies ran while one was open for 2% of the time, Pallas kernels for 0%

profile of v2, /device:TPU:1, one launch (start us, length us, event | category | flops | bytes accessed | tf_op | source)
XLA Modules:
  0.0 212.5 jit_solution(10850738834172643733)
XLA Ops:
  7.2 0.0 copy-start.2
  7.2 0.0 all-gather.3.cloned.1.call-start
  7.2 0.9 reshape.86
  8.2 1.0 broadcast_select_fusion
  9.2 0.2 reshape.85
  9.4 0.1 fusion
  9.5 0.2 pad_maximum_fusion.1
  9.7 0.8 copy.17
  10.6 0.0 all-gather.3.cloned.1.call-update
  10.6 0.0 copy-done.2
  10.6 0.1 copy.20
  10.7 11.9 %all_to_all.25 = bf16[8,64,144]{2,1,0:T(8,128)(2,1)S(1)} all-to-all(bf16[8,64,144]{2,1,0:T(8,128)(2,1)S(1)} %bitcast.38), channel_id=1, replica_groups=mesh['z'=8,'yh'=2,'core'=2,'yl'=2,'x'=4] {'yl','x'}, dimensions={0} | all-to-all | bytes 294912 | tf_op jit(solution)/shard_map/all_to_all | solution.py:197
  22.7 0.1 copy.19
  22.8 0.3 broadcast_in_dim.10
  23.1 0.1 broadcast_in_dim.11
  23.3 36.5 %all_to_all.26 = bf16[8,64,1152]{2,1,0:T(8,128)(2,1)S(1)} all-to-all(bf16[8,64,1152]{2,1,0:T(8,128)(2,1)S(1)} %broadcast_in_dim.11), channel_id=1, replica_groups=mesh['z'=8,'yh'=2,'core'=2,'yl'=2,'x'=4] {'z'}, dimensions={0} | all-to-all | bytes 2359296 | tf_op jit(solution)/shard_map/all_to_all | solution.py:24
  59.8 4.0 %collective-permute-start = (bf16[512,1152]{1,0:T(8,128)(2,1)S(1)}, bf16[512,1152]{1,0:T(8,128)(2,1)S(1)}, u32[]{:S(2)}, u32[]{:S(2)}) collective-permute-start(bf16[512,1152]{1,0:T(8,128)(2,1)S(1)} %bitcast.35), channel_id=1, source_target_pairs={{0,8},{8,0},{1,9},{9,1},{2,10},{10,2},{3,11},{11,3},{4,12},{12,4},... | collective-permute-start | bytes 3538952 | tf_op jit(solution)/shard_map/ppermute | solution.py:199
  65.0 0.7 pad_maximum_fusion.2.scalars
  65.7 0.6 pad_add_fusion.1.info
  66.3 0.6 pad_add_fusion
  66.9 0.0 collective-permute-done.text_b
  66.9 9.6 %all-gather.3.cloned.1.call-done = bf16[144,144,128]{2,1,0:T(8,128)(2,1)} async-done(((bf16[9,144,128]{2,1,0:T(8,128)(2,1)}), bf16[144,144,128]{2,1,0:T(8,128)(2,1)}) %all-gather.3.cloned.1.call-update) | async-done | bytes 5308432 | tf_op jit(solution)/shard_map/all_gather | solution.py:194
  76.6 2.0 slice.36
  78.6 0.0 copy-done.1
  78.6 0.0 copy-done.3
  78.6 0.8 collective-permute-start.1
  79.4 5.1 %collective-permute-done.1.other = bf16[16,5,144,128]{3,2,1,0:T(8,128)(2,1)} collective-permute-done((bf16[16,5,144,128]{3,2,1,0:T(8,128)(2,1)S(1)}, bf16[16,5,144,128]{3,2,1,0:T(8,128)(2,1)}, u32[]{:S(2)}, u32[]{:S(2)}) %collective-permute-start.1) | collective-permute-done | bytes 2949152 | tf_op jit(solution)/shard_map/ppermute | solution.py:210
  84.5 30.2 %block.1 = (bf16[1152,1152]{1,0:T(8,128)(2,1)}, bf16[1152,1152]{1,0:T(8,128)(2,1)}, f32[1,1024]{1,0:T(1,128)}) custom-call(s32[3]{0:T(128)} %pad_add_fusion.1.info, f32[3]{0:T(128)} %pad_maximum_fusion.2.scalars, s32[1,1024]{1,0:T(1,128)} %bitcast.42, bf16[16,9,144,128]{3,2,1,0:T(8,128)(2,1)} %bitcast.29, ...), custom_call_target="tpu_custom_call" | custom-call | flops 18119393280 | bytes 20971520 | tf_op jit(solution)/shard_map/block/pallas_call | solution.py:216
  114.7 0.5 collective-permute-start.2
  115.2 0.7 broadcast_select_fusion.1
  116.0 2.7 %collective-permute-start.3 = (f32[512]{0:T(512)S(1)}, f32[512]{0:T(512)S(1)}, u32[]{:S(2)}, u32[]{:S(2)}) collective-permute-start(f32[512]{0:T(512)S(1)} %bitcast.43), channel_id=1, source_target_pairs={{0,16},{16,0},{1,17},{17,1},{2,18},{18,2},{3,19},{19,3},{4,20},{20... | collective-permute-start | bytes 6152 | tf_op jit(solution)/shard_map/ppermute | solution.py:253
  118.6 1.3 collective-permute-done.3
  120.0 0.1 collective-permute-done.2
  120.0 2.5 %add_convert_fusion = bf16[1152,1152]{1,0:T(8,128)(2,1)S(1)} fusion(bf16[1152,1152]{1,0:T(8,128)(2,1)S(1)} %collective-permute-done.2, bf16[1152,1152]{1,0:T(8,128)(2,1)} %get-tuple-element.18), kind=kLoop, calls=%fused_computation.1 | loop fusion | flops 5308416 | bytes 7962624 | tf_op jit(solution)/shard_map/convert_element_type | solution.py:257
  122.5 0.2 pad_maximum_fusion
  122.8 36.5 %all_to_all.27 = bf16[8,152,1152]{2,1,0:T(8,128)(2,1)S(1)} all-to-all(bf16[8,152,1152]{2,1,0:T(8,128)(2,1)S(1)} %pad_maximum_fusion), channel_id=1, replica_groups=mesh['z'=8,'yh'=2,'core'=2,'yl'=2,'x'=4] {'yl','x'}, dimensions={0} | all-to-all | bytes 5603328 | tf_op jit(solution)/shard_map/all_to_all | solution.py:260
  159.2 0.4 convert_element_type.42
  159.6 0.0 copy-start
  159.6 0.2 slice_reduce_fusion
  159.9 2.2 %copy-done = f32[8,152,1152]{2,1,0:T(8,128)} copy-done((f32[8,152,1152]{2,1,0:T(8,128)}, f32[8,152,1152]{2,1,0:T(8,128)S(1)}, u32[]{:S(2)}) %copy-start) | copy-done | bytes 5603352
  162.1 20.3 %all_to_all.28 = bf16[16,88,128]{2,1,0:T(8,128)(2,1)S(1)} all-to-all(bf16[16,88,128]{2,1,0:T(8,128)(2,1)S(1)} %bitcast.30), channel_id=1, replica_groups=mesh['z'=8,'yh'=2,'core'=2,'yl'=2,'x'=4] {'z','yh'}, dimensions={0} | all-to-all | bytes 720896 | tf_op jit(solution)/shard_map/all_to_all | solution.py:270
  182.4 0.1 reduce_sum.31
  182.5 15.8 %all_to_all.29 = bf16[16,88,128]{2,1,0:T(8,128)(2,1)S(1)} all-to-all(bf16[16,88,128]{2,1,0:T(8,128)(2,1)S(1)} %broadcast_in_dim.27), channel_id=1, replica_groups=mesh['z'=8,'yh'=2,'core'=2,'yl'=2,'x'=4] {'z','yh'}, dimensions={0} | all-to-all | bytes 720896 | tf_op jit(solution)/shard_map/all_to_all | solution.py:24
  198.3 4.6 %collective-permute-start.4 = (bf16[144,1152]{1,0:T(8,128)(2,1)S(1)}, bf16[144,1152]{1,0:T(8,128)(2,1)S(1)}, u32[]{:S(2)}, u32[]{:S(2)}) collective-permute-start(bf16[144,1152]{1,0:T(8,128)(2,1)S(1)} %bitcast.33), channel_id=1, source_target_pairs={{0,8},{8,0},{1,9},{9,1},{2,10},{10,2},{3,11},{11,3},{4,12},{12,4},... | collective-permute-start | bytes 995336 | tf_op jit(solution)/shard_map/ppermute | solution.py:274
  202.9 1.0 slice_reduce_fusion.1
  203.9 0.6 fusion.16
  204.5 0.0 collective-permute-done.4
  204.5 1.1 select_convert_fusion
  (11 shorter events, 0.2 us)
Async XLA Ops:
  7.2 3.4 %copy-start.2 = (bf16[512,144]{0,1:T(8,128)(2,1)S(1)}, bf16[512,144]{0,1:T(8,128)(2,1)}, u32[]{:S(2)}) copy-start(bf16[512,144]{0,1:T(8,128)(2,1)} %param.7) | copy-start | bytes 442372
  7.2 69.4 %all-gather.3.cloned.1.call-start = ((), (), s32[]{:S(2)}) async-start(), calls=%async_computation.5 | async-start | bytes 5640192 | tf_op jit(solution)/shard_map/all_gather | solution.py:194
  59.8 18.8 %copy-start.1 = (bf16[8,64,1152]{2,1,0:T(8,128)(2,1)}, bf16[8,64,1152]{2,1,0:T(8,128)(2,1)S(1)}, u32[]{:S(2)}) copy-start(bf16[8,64,1152]{2,1,0:T(8,128)(2,1)S(1)} %all_to_all.26) | copy-start | bytes 3538948
  59.8 7.2 %collective-permute-start = (bf16[512,1152]{1,0:T(8,128)(2,1)S(1)}, bf16[512,1152]{1,0:T(8,128)(2,1)S(1)}, u32[]{:S(2)}, u32[]{:S(2)}) collective-permute-start(bf16[512,1152]{1,0:T(8,128)(2,1)S(1)} %bitcast.35), channel_id=1, source_target_pairs={{0,8},{8,0},{1,9},{9,1},{2,10},{10,2},{3,11},{11,3},{4,12},{12,4},... | collective-permute-start | bytes 3538952 | tf_op jit(solution)/shard_map/ppermute | solution.py:199
  66.9 11.7 %copy-start.3 = (bf16[512,1152]{1,0:T(8,128)(2,1)}, bf16[512,1152]{1,0:T(8,128)(2,1)S(1)}, u32[]{:S(2)}) copy-start(bf16[512,1152]{1,0:T(8,128)(2,1)S(1)} %collective-permute-done.text_b) | copy-start | bytes 3538948
  78.6 5.9 %collective-permute-start.1 = (bf16[16,5,144,128]{3,2,1,0:T(8,128)(2,1)S(1)}, bf16[16,5,144,128]{3,2,1,0:T(8,128)(2,1)}, u32[]{:S(2)}, u32[]{:S(2)}) collective-permute-start(bf16[16,5,144,128]{3,2,1,0:T(8,128)(2,1)S(1)} %slice.36), channel_id=1, source_target_pairs={{0,8},{8,0},{1,9},{9,1},{2,10},{10,2},{3,11},{11,3},{4,12},{12,4},... | collective-permute-start | bytes 8847368 | tf_op jit(solution)/shard_map/ppermute | solution.py:210
  114.7 5.3 %collective-permute-start.2 = (bf16[1152,1152]{1,0:T(8,128)(2,1)}, bf16[1152,1152]{1,0:T(8,128)(2,1)S(1)}, u32[]{:S(2)}, u32[]{:S(2)}) collective-permute-start(bf16[1152,1152]{1,0:T(8,128)(2,1)} %get-tuple-element.19), channel_id=1, source_target_pairs={{0,8},{8,0},{1,9},{9,1},{2,10},{10,2},{3,11},{11,3},{4,12},{12,4},... | collective-permute-start | bytes 7962632 | tf_op jit(solution)/shard_map/ppermute | solution.py:257
  116.0 4.0 %collective-permute-start.3 = (f32[512]{0:T(512)S(1)}, f32[512]{0:T(512)S(1)}, u32[]{:S(2)}, u32[]{:S(2)}) collective-permute-start(f32[512]{0:T(512)S(1)} %bitcast.43), channel_id=1, source_target_pairs={{0,16},{16,0},{1,17},{17,1},{2,18},{18,2},{3,19},{19,3},{4,20},{20... | collective-permute-start | bytes 6152 | tf_op jit(solution)/shard_map/ppermute | solution.py:253
  159.6 2.4 %copy-start = (f32[8,152,1152]{2,1,0:T(8,128)}, f32[8,152,1152]{2,1,0:T(8,128)S(1)}, u32[]{:S(2)}) copy-start(f32[8,152,1152]{2,1,0:T(8,128)S(1)} %convert_element_type.42) | copy-start | bytes 16809988
  198.3 6.1 %collective-permute-start.4 = (bf16[144,1152]{1,0:T(8,128)(2,1)S(1)}, bf16[144,1152]{1,0:T(8,128)(2,1)S(1)}, u32[]{:S(2)}, u32[]{:S(2)}) collective-permute-start(bf16[144,1152]{1,0:T(8,128)(2,1)S(1)} %bitcast.33), channel_id=1, source_target_pairs={{0,8},{8,0},{1,9},{9,1},{2,10},{10,2},{3,11},{11,3},{4,12},{12,4},... | collective-permute-start | bytes 995336 | tf_op jit(solution)/shard_map/ppermute | solution.py:274
Sparse Core Ops, SparseCore 0:
  11.0 65.4 all-gather.2

commit v3 on v2

--- a/solution.py
+++ b/solution.py
@@ -56,7 +56,7 @@
 
 def block_kernel(
     low, info, scalars, ids, packed, other, text_a, text_b,
-    keep, give, loss,
+    keep_a, keep_b, give_a, give_b, loss,
     head_i, head_t, image, texts, raw_t, unit_t, unit_i, weight, backs, part_i, part_t, sems, out_sems,
 ):
     nt, depth, width = head_i.shape
@@ -137,18 +137,33 @@
 
     step = 3 * LANE
 
-    def out_copy(src, dst, at, k):
+    keep, give = (keep_a, keep_b), (give_a, give_b)
+    ny, _, cut = keep_a.shape
+
+    def out_copies(src, dst, at, k):
         here = pl.ds(k * step, step)
-        return pltpu.make_async_copy(src.at[here], dst.at[here], out_sems.at[at + k])
+        at = at + k * (ny + 1)
+        return [
+            pltpu.make_async_copy(
+                src.at[here, pl.ds(y * cut, cut)], dst[0].at[y, here], out_sems.at[at + y]
+            )
+            for y in range(ny)
+        ] + [
+            pltpu.make_async_copy(
+                src.at[here, pl.ds(ny * cut, width - ny * cut)], dst[1].at[here], out_sems.at[at + ny]
+            )
+        ]
 
     def send(src, at, mine, k):
         @pl.when(core == mine)
         def _():
-            out_copy(src, keep, at, k).start()
+            for copy in out_copies(src, keep, at, k):
+                copy.start()
 
         @pl.when(core != mine)
         def _():
-            out_copy(src, give, at, k).start()
+            for copy in out_copies(src, give, at, k):
+                copy.start()
 
     wide = nt // 2 * depth
     for k in range(2):
@@ -165,11 +180,13 @@
     for k in range(full // step):
         here = pl.ds(k * step, step)
         part_t[here] = contract(texts[:, here], backs[...], (0, 0)).astype(BF)
-        send(part_t, full // step, 1, k)
+        send(part_t, full // step * (ny + 1), 1, k)
 
     for k in range(full // step):
-        out_copy(part_i, keep, 0, k).wait()
-        out_copy(part_t, give, full // step, k).wait()
+        for copy in out_copies(part_i, keep, 0, k):
+            copy.wait()
+        for copy in out_copies(part_t, give, full // step * (ny + 1), k):
+            copy.wait()
 
 
 def on_device(image_feat, text_feat, image_head, text_head, logit_scale, logit_bias):
@@ -191,7 +208,9 @@
     head = jnp.where(core == 0, image_head, text_head).reshape(depth, nb, LANE)
     head = jnp.where(yh == 0, head[:, :low], head[:, nb - low :]).transpose(1, 0, 2)
     columns = image_feat.T.reshape(depth, pairs // LANE, LANE).transpose(1, 0, 2)
-    packed = lax.all_gather(jnp.concatenate([head, columns], axis=0), PLANE, axis=0)
+    packed = jnp.concatenate([head, columns], axis=0)
+    packed, text_feat = lax.optimization_barrier((packed, text_feat))
+    packed = lax.all_gather(packed, PLANE, axis=0)
 
     split = text_feat.reshape(nt, rows, depth)
     own = lax.all_to_all(split, T, 0, 0, tiled=True).transpose(1, 0, 2).reshape(rows, full)
@@ -213,15 +232,20 @@
     smem = pl.BlockSpec(memory_space=pltpu.SMEM)
     vmem = pl.BlockSpec(memory_space=pltpu.VMEM)
     hbm = pl.BlockSpec(memory_space=pl.ANY)
-    keep, give, losses = pl.pallas_call(
+    cut = width // LANE // 3 * LANE
+    sums = [
+        jax.ShapeDtypeStruct((ny, full, cut), BF),
+        jax.ShapeDtypeStruct((full, width - ny * cut), BF),
+    ]
+    keep_a, keep_b, give_a, give_b, losses = pl.pallas_call(
         functools.partial(block_kernel, low),
         out_shape=[
-            jax.ShapeDtypeStruct((full, width), BF),
-            jax.ShapeDtypeStruct((full, width), BF),
+            *sums,
+            *sums,
             jax.ShapeDtypeStruct((1, ni), F32),
         ],
         in_specs=[smem, smem, vmem, hbm, hbm, hbm, hbm],
-        out_specs=[hbm, hbm, vmem],
+        out_specs=[hbm, hbm, hbm, hbm, vmem],
         scratch_shapes=[
             pltpu.VMEM((nt, depth, width), BF),
             pltpu.VMEM((nt, depth, width), BF),
@@ -235,7 +259,7 @@
             pltpu.VMEM((full, width), BF),
             pltpu.VMEM((full, width), BF),
             pltpu.SemaphoreType.DMA((2 * nb + 2 + ni // LANE,)),
-            pltpu.SemaphoreType.DMA((2 * (full // (3 * LANE)),)),
+            pltpu.SemaphoreType.DMA((2 * (full // (3 * LANE)) * (ny + 1),)),
         ],
         compiler_params=pltpu.CompilerParams(vmem_limit_bytes=LIMIT),
         cost_estimate=pl.CostEstimate(
@@ -246,31 +270,70 @@
         name="block",
     )(info, scalars, ids, packed, other, text_a, text_b)
 
-    low_y = yh == 0
-    losses = losses.reshape(ny, pairs)
-    loss_mine = jnp.where(low_y, losses[0], losses[1])
-    loss_give = jnp.where(low_y, losses[1], losses[0])
-    loss = loss_mine + lax.ppermute(loss_give, "yh", SWAP)
-    head_part = lax.reduce_precision(loss, 8, 7)
-    row = jnp.concatenate([head_part, loss - head_part]).astype(BF)
-    row = jnp.pad(row[None], ((0, 7), (0, width - 2 * pairs)))
-    mine = (keep.astype(F32) + lax.ppermute(give, "core", SWAP).astype(F32)).astype(BF)
-    mine = mine.reshape(nt, depth, width)
-    mine = jnp.concatenate([mine, jnp.broadcast_to(row[None], (nt,) + row.shape)], axis=1)
-    mine = lax.all_to_all(mine, T, 0, 0, tiled=True).astype(F32)
-    row = jnp.sum(mine[:, depth], axis=0)
-    row_loss = (row[:pairs] + row[pairs : 2 * pairs]) / batch
-    one = jnp.sum(mine[:, :depth], axis=0).astype(BF)
-
-    n = nz * ny
-    tiles = (depth // 8) * nb
-    per = -(-tiles // n)
-    one = one.reshape(depth // 8, 8, nb, LANE).transpose(0, 2, 1, 3)
-    one = jnp.pad(one.reshape(tiles, 8, LANE), ((0, per * n - tiles), (0, 0), (0, 0)))
-    one = lax.all_to_all(one.reshape(n, per * 8, LANE), ZY, 0, 0, tiled=True)
+    nx, nyl = lax.axis_size("x"), lax.axis_size("yl")
+    n_y = ny * nyl
+    x = lax.axis_index("x")
+    half = depth // 2
+
+    def two_parts(loss):
+        first = lax.reduce_precision(loss, 8, 7)
+        parts = jnp.concatenate([first, loss - first], axis=-1).astype(BF)
+        spare = 8 * cut - 2 * pairs
+        parts = jnp.pad(parts, [(0, 0)] * (parts.ndim - 1) + [(0, spare)])
+        return parts.reshape(parts.shape[:-1] + (8, cut))
+
+    def one_part(rows):
+        return jnp.sum(rows.reshape(8 * cut)[: 2 * pairs].reshape(2, pairs), axis=0)
+
+    def over_x(chunk):
+        total = chunk(x).astype(F32)
+        for k in range(1, nx):
+            part = chunk(lax.rem(x + k, nx)).astype(BF)
+            total = total + lax.ppermute(part, "x", [(i, (i + k) % nx) for i in range(nx)]).astype(F32)
+        return total
+
+    def core_sum(mine, other):
+        return (mine.astype(F32) + lax.ppermute(other, "core", SWAP).astype(F32)).astype(BF)
+
+    a = core_sum(keep_a, give_a).reshape(ny, nyl, nx * depth, cut)
+    row = jnp.broadcast_to(two_parts(losses.reshape(ny, pairs))[:, None], (ny, nyl, 8, cut))
+    a = jnp.concatenate([a, row], axis=2).reshape(n_y, nx * depth + 8, cut)
+    a = lax.all_to_all(a, ("yh", "yl"), 0, 0, tiled=True)
+    b = core_sum(keep_b, give_b).reshape(nyl, nx, depth, width - ny * cut)
+    b = over_x(lambda k: lax.dynamic_index_in_dim(b, k, 1, keepdims=False)).astype(BF)
+
+    a, b = lax.optimization_barrier((a, b))
+    a = jnp.sum(a.astype(F32), axis=0)
+    row = two_parts(one_part(a[nx * depth :])).astype(F32)
+    a = a[: nx * depth].reshape(nx, depth, cut)
+    a = over_x(
+        lambda k: jnp.concatenate([lax.dynamic_index_in_dim(a, k, 0, keepdims=False), row], axis=0)
+    )
+    row_loss = one_part(a[depth:]) / batch
+    a = a[:depth].astype(BF)
+    b = b.reshape(nyl, ny, half, width - ny * cut).transpose(1, 0, 2, 3)
+    b = lax.all_to_all(b.reshape(n_y, half, width - ny * cut), ("yh", "yl"), 0, 0, tiled=True)
+    b = jnp.sum(b.astype(F32), axis=0).astype(BF)
+
+    def to_tiles(v):
+        r, c = v.shape
+        return v.reshape(r // 8, 8, c // LANE, LANE).transpose(0, 2, 1, 3).reshape(-1, 8, LANE)
+
+    def from_tiles(v, r, c):
+        return v.reshape(r // 8, c // LANE, 8, LANE).transpose(0, 2, 1, 3).reshape(r, c)
+
+    tiles_a = depth // 8 * (cut // LANE)
+    one = jnp.concatenate([to_tiles(a), to_tiles(b)], axis=0)
+    tiles = one.shape[0]
+    per = -(-tiles // nz)
+    one = jnp.pad(one, ((0, per * nz - tiles), (0, 0), (0, 0)))
+    one = lax.all_to_all(one.reshape(nz, per * 8, LANE), "z", 0, 0, tiled=True)
     one = jnp.sum(one.astype(F32), axis=0).astype(BF)
-    one = spread(one, ZY, n).reshape(per * n, 8, LANE)[:tiles]
-    one = one.reshape(depth // 8, nb, 8, LANE).transpose(0, 2, 1, 3).reshape(depth, width)
+    one = spread(one, ZY, nz * ny).reshape(nz, ny, per * 8, LANE).transpose(1, 0, 2, 3)
+    one = one.reshape(ny, per * nz, 8, LANE)
+    left = [from_tiles(one[y, :tiles_a], depth, cut) for y in range(ny)]
+    right = [from_tiles(one[y, tiles_a:tiles], half, width - ny * cut) for y in range(ny)]
+    one = jnp.concatenate([*left, jnp.concatenate(right, axis=0)], axis=1)
     two = lax.ppermute(one, "core", SWAP)
     out_i = jnp.where(core == 0, one, two).astype(F32)
     out_t = jnp.where(core == 0, two, one).astype(F32)

time: 213 us -> 211 us (level)
  blocking collectives: 121 us -> 63.6 us
  waiting for transfers between devices: 16.1 us -> 48.6 us
  starting transfers between devices: 12.5 us -> 31.3 us
  other arithmetic: 10.1 us -> 12.8 us
    all_to_all x2 -> x1, blocking collectives: 56.8 us -> 15.1 us  [on_device(): one = lax.all_to_all(one.reshape(nz, per * 8, LANE), 'z', 0, 0, tiled=True)]
    all_to_all x0 -> x3, waiting for transfers between devices: none -> 21.7 us  [the longest x1 12 us: spread(): return lax.all_to_all(wide, axes, 0, 0, tiled=True)]
    all_to_all x2 -> x1, blocking collectives: 52.3 us -> 36.5 us  [spread(): return lax.all_to_all(wide, axes, 0, 0, tiled=True)]
    all_to_all x0 -> x3, starting transfers between devices: none -> 10.9 us  [the longest x1 3.95 us: on_device(): a = lax.all_to_all(a, ('yh', 'yl'), 0, 0, tiled=True)]
    ppermute x2 -> x8, waiting for transfers between devices: 1.35 us -> 10.5 us  [the longest x6 8.99 us: over_x(): lax.ppermute(part, 'x', [(i, (i + k) % nx) for i in range(nx)]).astype(F32)]
    ppermute x2 -> x8, starting transfers between devices: 3.2 us -> 10.1 us  [the longest x6 9.46 us: over_x(): lax.ppermute(part, 'x', [(i, (i + k) % nx) for i in range(nx)]).astype(F32)]
    convert_element_type x2 -> x4, other arithmetic: 2.84 us -> 4.62 us  [the longest x2 3.56 us: core_sum(): (mine.astype(F32) + lax.ppermute(other, 'core', SWAP).astype(F32)).astype...]
  transfers between devices with their start and end apart: 6 -> 15, of which waited for: 4 -> 9; matrix products, arithmetic and copies ran while one was open for 2% -> 6% of each run, Pallas kernels for 0% -> 0%
where the time goes in v3:
time: 211 us; the launch traced here: 210 us
  blocking collectives  63.6 us (30%)
  waiting for transfers between devices  48.6 us (23%)
  starting transfers between devices  31.3 us (15%)
  Pallas kernels  30.3 us (14%)
  between operations  15.7 us (7%)
  other arithmetic  12.8 us (6%)
  local copies, waits for them, and re-layouts  7.81 us (4%)
    all_to_all x1, blocking collectives, spread(): return lax.all_to_all(wide, axes, 0, 0, tiled=True)  36.5 us
    pallas_call x1, Pallas kernels, on_device(): pl.pallas_call(functools.partial(block_kernel, low), out_shape=[*sums, *s...  30.3 us
    all_to_all x1, blocking collectives, on_device(): one = lax.all_to_all(one.reshape(nz, per * 8, LANE), 'z', 0, 0, tiled=True)  15.1 us
    all_to_all x1, waiting for transfers between devices, spread(): return lax.all_to_all(wide, axes, 0, 0, tiled=True)  12 us
    all_to_all x1, blocking collectives, on_device(): lax.all_to_all(split, T, 0, 0, tiled=True).transpose(1, 0, 2)  11.9 us
    all_gather x1, waiting for transfers between devices, on_device(): packed = lax.all_gather(packed, PLANE, axis=0)  10.6 us
    ppermute x6, starting transfers between devices, over_x(): lax.ppermute(part, 'x', [(i, (i + k) % nx) for i in range(nx)]).astype(F32)  9.46 us
    ppermute x6, waiting for transfers between devices, over_x(): lax.ppermute(part, 'x', [(i, (i + k) % nx) for i in range(nx)]).astype(F32)  8.99 us
  transfers between devices with their start and end apart: 15, of which 9 were waited for; matrix products, arithmetic and copies ran while one was open for 6% of the time, Pallas kernels for 0%

profile of v3, /device:TPU:1, one launch (start us, length us, event | category | flops | bytes accessed | tf_op | source)
XLA Modules:
  0.0 210.2 jit_solution(9474013411997819796)
XLA Ops:
  7.2 1.0 broadcast_select_fusion
  8.3 0.2 reshape.90
  8.6 0.2 pad_maximum_fusion.1
  8.9 0.8 copy.25
  9.9 11.9 %all_to_all.30 = bf16[8,64,144]{2,1,0:T(8,128)(2,1)S(1)} all-to-all(bf16[8,64,144]{2,1,0:T(8,128)(2,1)S(1)} %bitcast.91), channel_id=1, replica_groups=mesh['z'=8,'yh'=2,'core'=2,'yl'=2,'x'=4] {'yl','x'}, dimensions={0} | all-to-all | bytes 294912 | tf_op jit(solution)/shard_map/all_to_all | solution.py:216
  22.0 0.3 broadcast_in_dim.23
  22.4 36.5 %all_to_all.31 = bf16[8,64,1152]{2,1,0:T(8,128)(2,1)S(1)} all-to-all(bf16[8,64,1152]{2,1,0:T(8,128)(2,1)S(1)} %broadcast_in_dim.24), channel_id=1, replica_groups=mesh['z'=8,'yh'=2,'core'=2,'yl'=2,'x'=4] {'z'}, dimensions={0} | all-to-all | bytes 2359296 | tf_op jit(solution)/shard_map/all_to_all | solution.py:24
  58.9 4.0 %collective-permute-start = (bf16[512,1152]{1,0:T(8,128)(2,1)S(1)}, bf16[512,1152]{1,0:T(8,128)(2,1)S(1)}, u32[]{:S(2)}, u32[]{:S(2)}) collective-permute-start(bf16[512,1152]{1,0:T(8,128)(2,1)S(1)} %bitcast.88), channel_id=1, source_target_pairs={{0,8},{8,0},{1,9},{9,1},{2,10},{10,2},{3,11},{11,3},{4,12},{12,4},... | collective-permute-start | bytes 3538952 | tf_op jit(solution)/shard_map/ppermute | solution.py:218
  64.2 0.6 pad_maximum_fusion.5.scalars
  64.7 0.6 pad_add_fusion.1.info
  65.4 0.6 pad_add_fusion
  66.0 10.6 %all-gather.3.cloned.1.call-done = bf16[144,144,128]{2,1,0:T(8,128)(2,1)} async-done(((bf16[9,144,128]{2,1,0:T(8,128)(2,1)}), bf16[144,144,128]{2,1,0:T(8,128)(2,1)}) %all-gather.3.cloned.1.call-update) | async-done | bytes 5308432 | tf_op jit(solution)/shard_map/all_gather | solution.py:213
  76.6 2.0 slice.48
  78.6 0.8 collective-permute-start.1
  79.4 5.1 %collective-permute-done.1.other = bf16[16,5,144,128]{3,2,1,0:T(8,128)(2,1)} collective-permute-done((bf16[16,5,144,128]{3,2,1,0:T(8,128)(2,1)S(1)}, bf16[16,5,144,128]{3,2,1,0:T(8,128)(2,1)}, u32[]{:S(2)}, u32[]{:S(2)}) %collective-permute-start.1) | collective-permute-done | bytes 2949152 | tf_op jit(solution)/shard_map/ppermute | solution.py:229
  84.5 30.3 %block.1 = (bf16[2,1152,384]{2,1,0:T(8,128)(2,1)}, bf16[1152,384]{1,0:T(8,128)(2,1)}, bf16[2,1152,384]{2,1,0:T(8,128)(2,1)}, bf16[1152,384]{1,0:T(8,128)(2,1)}, f32[1,1024]{1,0:T(1,128)}) custom-call(s32[3]{0:T(128)} %pad_add_fusion.1.info, f32[3]{0:T(128)} %pad_maximum_fusion.5.scalars, s32[1,1024]{1,0:T(1,128)} %bitcast.109, ...), custom_call_target="tpu_custom_call" | custom-call | flops 18119393280 | bytes 20971520 | tf_op jit(solution)/shard_map/block/pallas_call | solution.py:240
  114.9 0.4 collective-permute-start.2
  115.4 0.5 broadcast.68
  116.0 1.3 reduce.5
  117.4 1.5 collective-permute-done.2
  118.8 1.9 add_convert_fusion
  120.8 1.4 pad_maximum_fusion
  122.2 3.9 %all-to-all-start.2 = ((bf16[4,584,384]{2,1,0:T(8,128)(2,1)}), bf16[4,584,384]{2,1,0:T(8,128)(2,1)S(1)}, u32[]{:S(2)}, u32[]{:S(2)}) async-start(bf16[4,584,384]{2,1,0:T(8,128)(2,1)} %pad_maximum_fusion), calls=%async_computation.2 | async-start | bytes 3588096 | tf_op jit(solution)/shard_map/all_to_all | solution.py:301
  126.2 0.9 copy-done.1
  127.1 1.7 add_convert_fusion.1
  128.8 0.9 dynamic-slice_bitcast_fusion.3
  129.6 0.9 collective-permute-start.4
  130.5 2.4 %collective-permute-start.5 = (bf16[2,144,384]{2,1,0:T(8,128)(2,1)}, bf16[2,144,384]{2,1,0:T(8,128)(2,1)S(1)}, u32[]{:S(2)}, u32[]{:S(2)}) collective-permute-start(bf16[2,144,384]{2,1,0:T(8,128)(2,1)} %get-tuple-element.38), channel_id=1, source_target_pairs={{0,2},{1,3},{2,0},{3,1},{4,6},{5,7},{6,4},{7,5},{8,10},{9,11},{10,... | collective-permute-start | bytes 663560 | tf_op jit(solution)/shard_map/ppermute | solution.py:292
  132.9 1.2 collective-permute-start.6
  134.0 3.3 %collective-permute-done.4 = bf16[2,144,384]{2,1,0:T(8,128)(2,1)S(1)} collective-permute-done((bf16[2,144,384]{2,1,0:T(8,128)(2,1)}, bf16[2,144,384]{2,1,0:T(8,128)(2,1)S(1)}, u32[]{:S(2)}, u32[]{:S(2)}) %collective-permute-start.4) | collective-permute-done | bytes 221216 | tf_op jit(solution)/shard_map/ppermute | solution.py:292
  137.4 5.6 %collective-permute-done.5 = bf16[2,144,384]{2,1,0:T(8,128)(2,1)S(1)} collective-permute-done((bf16[2,144,384]{2,1,0:T(8,128)(2,1)}, bf16[2,144,384]{2,1,0:T(8,128)(2,1)S(1)}, u32[]{:S(2)}, u32[]{:S(2)}) %collective-permute-start.5) | collective-permute-done | bytes 221216 | tf_op jit(solution)/shard_map/ppermute | solution.py:292
  143.0 1.1 fusion.2
  144.1 4.6 %all-to-all-done.2 = bf16[4,584,384]{2,1,0:T(8,128)(2,1)S(1)} async-done(((bf16[4,584,384]{2,1,0:T(8,128)(2,1)}), bf16[4,584,384]{2,1,0:T(8,128)(2,1)S(1)}, u32[]{:S(2)}, u32[]{:S(2)}) %all-to-all-start.2) | async-done | bytes 1794080 | tf_op jit(solution)/shard_map/all_to_all | solution.py:301
  148.7 0.3 convert_reduce_fusion
  149.2 1.5 collective-permute-start.7
  150.7 2.4 %collective-permute-start.8 = (bf16[152,384]{1,0:T(8,128)(2,1)S(1)}, bf16[152,384]{1,0:T(8,128)(2,1)S(1)}, u32[]{:S(2)}, u32[]{:S(2)}) collective-permute-start(bf16[152,384]{1,0:T(8,128)(2,1)S(1)} %get-tuple-element.46), channel_id=1, source_target_pairs={{0,2},{1,3},{2,0},{3,1},{4,6},{5,7},{6,4},{7,5},{8,10},{9,11},{10,... | collective-permute-start | bytes 350216 | tf_op jit(solution)/shard_map/ppermute | solution.py:292
  153.1 1.2 collective-permute-start.9
  154.3 0.7 copy.29
  155.0 3.4 %all-to-all-start.3 = ((bf16[4,72,384]{2,1,0:T(8,128)(2,1)}), bf16[4,72,384]{2,1,0:T(8,128)(2,1)S(1)}, u32[]{:S(2)}, u32[]{:S(2)}) async-start(bf16[4,72,384]{2,1,0:T(8,128)(2,1)} %bitcast.28), calls=%async_computation.3 | async-start | bytes 442368 | tf_op jit(solution)/shard_map/all_to_all | solution.py:315
  158.5 5.1 %all-to-all-done.3 = bf16[4,72,384]{2,1,0:T(8,128)(2,1)S(1)} async-done(((bf16[4,72,384]{2,1,0:T(8,128)(2,1)}), bf16[4,72,384]{2,1,0:T(8,128)(2,1)S(1)}, u32[]{:S(2)}, u32[]{:S(2)}) %all-to-all-start.3) | async-done | bytes 221216 | tf_op jit(solution)/shard_map/all_to_all | solution.py:315
  163.7 15.1 %all_to_all.32 = bf16[8,88,128]{2,1,0:T(8,128)(2,1)S(1)} all-to-all(bf16[8,88,128]{2,1,0:T(8,128)(2,1)S(1)} %bitcast.97), channel_id=1, replica_groups=mesh['z'=8,'yh'=2,'core'=2,'yl'=2,'x'=4] {'z'}, dimensions={0} | all-to-all | bytes 360448 | tf_op jit(solution)/shard_map/all_to_all | solution.py:330
  178.8 0.8 broadcast_in_dim.28
  179.6 3.5 %all-to-all-start.5 = ((bf16[16,88,128]{2,1,0:T(8,128)(2,1)}), bf16[16,88,128]{2,1,0:T(8,128)(2,1)S(1)}, u32[]{:S(2)}, u32[]{:S(2)}) async-start(bf16[16,88,128]{2,1,0:T(8,128)(2,1)} %broadcast_in_dim.28), calls=%async_computation.5 | async-start | bytes 720896 | tf_op jit(solution)/shard_map/all_to_all | solution.py:24
  183.2 12.0 %all-to-all-done.5 = bf16[16,88,128]{2,1,0:T(8,128)(2,1)S(1)} async-done(((bf16[16,88,128]{2,1,0:T(8,128)(2,1)}), bf16[16,88,128]{2,1,0:T(8,128)(2,1)S(1)}, u32[]{:S(2)}, u32[]{:S(2)}) %all-to-all-start.5) | async-done | bytes 360480 | tf_op jit(solution)/shard_map/all_to_all | solution.py:24
  195.3 5.6 %collective-permute-start.10 = (bf16[144,1152]{1,0:T(8,128)(2,1)S(1)}, bf16[144,1152]{1,0:T(8,128)(2,1)S(1)}, u32[]{:S(2)}, u32[]{:S(2)}) collective-permute-start(bf16[144,1152]{1,0:T(8,128)(2,1)S(1)} %maximum_maximum_fusion), channel_id=1, source_target_pairs={{0,8},{8,0},{1,9},{9,1},{2,10},{10,2},{3,11},{11,3},{4,12},{12,4},... | collective-permute-start | bytes 995336 | tf_op jit(solution)/shard_map/ppermute | solution.py:337
  200.9 0.6 broadcast_multiply_fusion
  201.5 0.7 collective-permute-done.10
  202.2 1.2 select_convert_fusion
  (52 shorter events, 1.4 us)
Async XLA Ops:
  7.2 1.3 copy-start.3
  7.2 69.4 %all-gather.3.cloned.1.call-start = ((), (), s32[]{:S(2)}) async-start(), calls=%async_computation.6 | async-start | bytes 5640192 | tf_op jit(solution)/shard_map/all_gather | solution.py:213
  8.5 1.2 copy-start.2
  58.9 19.7 %copy-start = (bf16[8,64,1152]{2,1,0:T(8,128)(2,1)}, bf16[8,64,1152]{2,1,0:T(8,128)(2,1)S(1)}, u32[]{:S(2)}) copy-start(bf16[8,64,1152]{2,1,0:T(8,128)(2,1)S(1)} %all_to_all.31) | copy-start | bytes 3538948
  58.9 7.1 %collective-permute-start = (bf16[512,1152]{1,0:T(8,128)(2,1)S(1)}, bf16[512,1152]{1,0:T(8,128)(2,1)S(1)}, u32[]{:S(2)}, u32[]{:S(2)}) collective-permute-start(bf16[512,1152]{1,0:T(8,128)(2,1)S(1)} %bitcast.88), channel_id=1, source_target_pairs={{0,8},{8,0},{1,9},{9,1},{2,10},{10,2},{3,11},{11,3},{4,12},{12,4},... | collective-permute-start | bytes 3538952 | tf_op jit(solution)/shard_map/ppermute | solution.py:218
  66.0 12.6 %copy-start.4 = (bf16[512,1152]{1,0:T(8,128)(2,1)}, bf16[512,1152]{1,0:T(8,128)(2,1)S(1)}, u32[]{:S(2)}) copy-start(bf16[512,1152]{1,0:T(8,128)(2,1)S(1)} %collective-permute-done.text_b) | copy-start | bytes 3538948
  78.6 5.9 %collective-permute-start.1 = (bf16[16,5,144,128]{3,2,1,0:T(8,128)(2,1)S(1)}, bf16[16,5,144,128]{3,2,1,0:T(8,128)(2,1)}, u32[]{:S(2)}, u32[]{:S(2)}) collective-permute-start(bf16[16,5,144,128]{3,2,1,0:T(8,128)(2,1)S(1)} %slice.48), channel_id=1, source_target_pairs={{0,8},{8,0},{1,9},{9,1},{2,10},{10,2},{3,11},{11,3},{4,12},{12,4},... | collective-permute-start | bytes 8847368 | tf_op jit(solution)/shard_map/ppermute | solution.py:229
  114.9 4.0 %collective-permute-start.2 = (bf16[2,1152,384]{2,1,0:T(8,128)(2,1)}, bf16[2,1152,384]{2,1,0:T(8,128)(2,1)S(1)}, u32[]{:S(2)}, u32[]{:S(2)}) collective-permute-start(bf16[2,1152,384]{2,1,0:T(8,128)(2,1)} %get-tuple-element.27), channel_id=1, source_target_pairs={{0,8},{8,0},{1,9},{9,1},{2,10},{10,2},{3,11},{11,3},{4,12},{12,4},... | collective-permute-start | bytes 5308424 | tf_op jit(solution)/shard_map/ppermute | solution.py:296
  115.3 10.9 %collective-permute-start.3 = (bf16[1152,384]{1,0:T(8,128)(2,1)}, bf16[1152,384]{1,0:T(8,128)(2,1)S(1)}, u32[]{:S(2)}, u32[]{:S(2)}) collective-permute-start(bf16[1152,384]{1,0:T(8,128)(2,1)} %get-tuple-element.30), channel_id=1, source_target_pairs={{0,8},{8,0},{1,9},{9,1},{2,10},{10,2},{3,11},{11,3},{4,12},{12,4},... | collective-permute-start | bytes 2654216 | tf_op jit(solution)/shard_map/ppermute | solution.py:296
  122.2 26.5 %all-to-all-start.2 = ((bf16[4,584,384]{2,1,0:T(8,128)(2,1)}), bf16[4,584,384]{2,1,0:T(8,128)(2,1)S(1)}, u32[]{:S(2)}, u32[]{:S(2)}) async-start(bf16[4,584,384]{2,1,0:T(8,128)(2,1)} %pad_maximum_fusion), calls=%async_computation.2 | async-start | bytes 3588096 | tf_op jit(solution)/shard_map/all_to_all | solution.py:301
  126.2 0.9 copy-start.1
  129.6 7.8 %collective-permute-start.4 = (bf16[2,144,384]{2,1,0:T(8,128)(2,1)}, bf16[2,144,384]{2,1,0:T(8,128)(2,1)S(1)}, u32[]{:S(2)}, u32[]{:S(2)}) collective-permute-start(bf16[2,144,384]{2,1,0:T(8,128)(2,1)} %get-tuple-element.36), channel_id=1, source_target_pairs={{0,1},{1,2},{2,3},{3,0},{4,5},{5,6},{6,7},{7,4},{8,9},{9,10},{10,1... | collective-permute-start | bytes 663560 | tf_op jit(solution)/shard_map/ppermute | solution.py:292
  130.5 12.6 %collective-permute-start.5 = (bf16[2,144,384]{2,1,0:T(8,128)(2,1)}, bf16[2,144,384]{2,1,0:T(8,128)(2,1)S(1)}, u32[]{:S(2)}, u32[]{:S(2)}) collective-permute-start(bf16[2,144,384]{2,1,0:T(8,128)(2,1)} %get-tuple-element.38), channel_id=1, source_target_pairs={{0,2},{1,3},{2,0},{3,1},{4,6},{5,7},{6,4},{7,5},{8,10},{9,11},{10,... | collective-permute-start | bytes 663560 | tf_op jit(solution)/shard_map/ppermute | solution.py:292
  132.9 10.2 %collective-permute-start.6 = (bf16[2,144,384]{2,1,0:T(8,128)(2,1)S(1)}, bf16[2,144,384]{2,1,0:T(8,128)(2,1)}, u32[]{:S(2)}, u32[]{:S(2)}) collective-permute-start(bf16[2,144,384]{2,1,0:T(8,128)(2,1)S(1)} %get-tuple-element.37), channel_id=1, source_target_pairs={{0,3},{1,0},{2,1},{3,2},{4,7},{5,4},{6,5},{7,6},{8,11},{9,8},{10,9... | collective-permute-start | bytes 663560 | tf_op jit(solution)/shard_map/ppermute | solution.py:292
  149.2 9.2 %collective-permute-start.7 = (bf16[152,384]{1,0:T(8,128)(2,1)S(1)}, bf16[152,384]{1,0:T(8,128)(2,1)S(1)}, u32[]{:S(2)}, u32[]{:S(2)}) collective-permute-start(bf16[152,384]{1,0:T(8,128)(2,1)S(1)} %get-tuple-element.45), channel_id=1, source_target_pairs={{0,1},{1,2},{2,3},{3,0},{4,5},{5,6},{6,7},{7,4},{8,9},{9,10},{10,1... | collective-permute-start | bytes 350216 | tf_op jit(solution)/shard_map/ppermute | solution.py:292
  150.7 7.7 %collective-permute-start.8 = (bf16[152,384]{1,0:T(8,128)(2,1)S(1)}, bf16[152,384]{1,0:T(8,128)(2,1)S(1)}, u32[]{:S(2)}, u32[]{:S(2)}) collective-permute-start(bf16[152,384]{1,0:T(8,128)(2,1)S(1)} %get-tuple-element.46), channel_id=1, source_target_pairs={{0,2},{1,3},{2,0},{3,1},{4,6},{5,7},{6,4},{7,5},{8,10},{9,11},{10,... | collective-permute-start | bytes 350216 | tf_op jit(solution)/shard_map/ppermute | solution.py:292
  153.1 5.3 %collective-permute-start.9 = (bf16[152,384]{1,0:T(8,128)(2,1)S(1)}, bf16[152,384]{1,0:T(8,128)(2,1)S(1)}, u32[]{:S(2)}, u32[]{:S(2)}) collective-permute-start(bf16[152,384]{1,0:T(8,128)(2,1)S(1)} %get-tuple-element.47), channel_id=1, source_target_pairs={{0,3},{1,0},{2,1},{3,2},{4,7},{5,4},{6,5},{7,6},{8,11},{9,8},{10,9... | collective-permute-start | bytes 350216 | tf_op jit(solution)/shard_map/ppermute | solution.py:292
  155.0 8.7 %all-to-all-start.3 = ((bf16[4,72,384]{2,1,0:T(8,128)(2,1)}), bf16[4,72,384]{2,1,0:T(8,128)(2,1)S(1)}, u32[]{:S(2)}, u32[]{:S(2)}) async-start(bf16[4,72,384]{2,1,0:T(8,128)(2,1)} %bitcast.28), calls=%async_computation.3 | async-start | bytes 442368 | tf_op jit(solution)/shard_map/all_to_all | solution.py:315
  179.6 15.6 %all-to-all-start.5 = ((bf16[16,88,128]{2,1,0:T(8,128)(2,1)}), bf16[16,88,128]{2,1,0:T(8,128)(2,1)S(1)}, u32[]{:S(2)}, u32[]{:S(2)}) async-start(bf16[16,88,128]{2,1,0:T(8,128)(2,1)} %broadcast_in_dim.28), calls=%async_computation.5 | async-start | bytes 720896 | tf_op jit(solution)/shard_map/all_to_all | solution.py:24
  195.3 6.9 %collective-permute-start.10 = (bf16[144,1152]{1,0:T(8,128)(2,1)S(1)}, bf16[144,1152]{1,0:T(8,128)(2,1)S(1)}, u32[]{:S(2)}, u32[]{:S(2)}) collective-permute-start(bf16[144,1152]{1,0:T(8,128)(2,1)S(1)} %maximum_maximum_fusion), channel_id=1, source_target_pairs={{0,8},{8,0},{1,9},{9,1},{2,10},{10,2},{3,11},{11,3},{4,12},{12,4},... | collective-permute-start | bytes 995336 | tf_op jit(solution)/shard_map/ppermute | solution.py:337
Sparse Core Ops, SparseCore 0:
  11.0 65.4 all-gather.2

commit v4 on v3

--- a/solution.py
+++ b/solution.py
@@ -92,18 +92,19 @@
             for copy in head_copies(other, dst, at, low):
                 copy.start()
 
-    for copy in text_copies:
-        copy.start()
+    text_copies[0].start()
     start_head(head_t, sems_t, 1)
-    for copy in text_copies + head_copies(packed, head_t, sems_t, low):
+    for copy in text_copies[:1] + head_copies(packed, head_t, sems_t, low):
         copy.wait()
+    text_copies[1].start()
     start_head(head_i, sems_i, 0)
     for copy in image_copies:
         copy.start()
 
-    @pl.loop(0, nj // TILE)
-    def _(j):
-        here = pl.ds(pl.multiple_of(j * TILE, TILE), TILE)
+    for j in range(nj // TILE):
+        if j * TILE == nj // 2:
+            text_copies[1].wait()
+        here = pl.ds(j * TILE, TILE)
         raw = contract(texts[here], head_t[...].reshape(full, width), (1, 0))
         raw_t[here] = raw
         unit_t[here] = (raw * stats(raw)[0]).astype(BF)
@@ -285,11 +286,12 @@
     def one_part(rows):
         return jnp.sum(rows.reshape(8 * cut)[: 2 * pairs].reshape(2, pairs), axis=0)
 
-    def over_x(chunk):
-        total = chunk(x).astype(F32)
-        for k in range(1, nx):
-            part = chunk(lax.rem(x + k, nx)).astype(BF)
-            total = total + lax.ppermute(part, "x", [(i, (i + k) % nx) for i in range(nx)]).astype(F32)
+    def over(axes, n, at, chunk):
+        total = chunk(at).astype(F32)
+        for k in range(1, n):
+            part = chunk(lax.rem(at + k, n)).astype(BF)
+            part = lax.ppermute(part, axes, [(i, (i + k) % n) for i in range(n)])
+            total = total + part.astype(F32)
         return total
 
     def core_sum(mine, other):
@@ -300,20 +302,20 @@
     a = jnp.concatenate([a, row], axis=2).reshape(n_y, nx * depth + 8, cut)
     a = lax.all_to_all(a, ("yh", "yl"), 0, 0, tiled=True)
     b = core_sum(keep_b, give_b).reshape(nyl, nx, depth, width - ny * cut)
-    b = over_x(lambda k: lax.dynamic_index_in_dim(b, k, 1, keepdims=False)).astype(BF)
-
-    a, b = lax.optimization_barrier((a, b))
+    b = over("x", nx, x, lambda k: lax.dynamic_index_in_dim(b, k, 1, keepdims=False)).astype(BF)
+    b = b.reshape(nyl, ny, half, width - ny * cut).transpose(1, 0, 2, 3).reshape(n_y, half, -1)
+    at_y = lax.axis_index(("yh", "yl"))
+    b = over(("yh", "yl"), n_y, at_y, lambda k: lax.dynamic_index_in_dim(b, k, 0, keepdims=False))
+
     a = jnp.sum(a.astype(F32), axis=0)
     row = two_parts(one_part(a[nx * depth :])).astype(F32)
     a = a[: nx * depth].reshape(nx, depth, cut)
-    a = over_x(
-        lambda k: jnp.concatenate([lax.dynamic_index_in_dim(a, k, 0, keepdims=False), row], axis=0)
+    a = over(
+        "x", nx, x, lambda k: jnp.concatenate([lax.dynamic_index_in_dim(a, k, 0, keepdims=False), row], axis=0)
     )
     row_loss = one_part(a[depth:]) / batch
     a = a[:depth].astype(BF)
-    b = b.reshape(nyl, ny, half, width - ny * cut).transpose(1, 0, 2, 3)
-    b = lax.all_to_all(b.reshape(n_y, half, width - ny * cut), ("yh", "yl"), 0, 0, tiled=True)
-    b = jnp.sum(b.astype(F32), axis=0).astype(BF)
+    b = b.astype(BF)
 
     def to_tiles(v):
         r, c = v.shape

time: 211 us -> 208 us (0.986)
  waiting for transfers between devices: 48.6 us -> 45.5 us
    ppermute x6 -> x9, waiting for transfers between devices: 8.99 us -> 15.6 us  [over(): part = lax.ppermute(part, axes, [(i, (i + k) % n) for i in range(n)])]
    all_to_all x1 -> x0, waiting for transfers between devices: 5.12 us -> none  [on_device(): lax.all_to_all(b.reshape(n_y, half, width - ny * cut), ('yh', 'yl'), 0, 0...]
    all_to_all x1, waiting for transfers between devices: 4.62 us -> 0.01 us  [on_device(): a = lax.all_to_all(a, ('yh', 'yl'), 0, 0, tiled=True)]
    ppermute x6 -> x9, starting transfers between devices: 9.46 us -> 13.8 us  [over(): part = lax.ppermute(part, axes, [(i, (i + k) % n) for i in range(n)])]
    all_to_all x1 -> x0, starting transfers between devices: 3.38 us -> none  [on_device(): lax.all_to_all(b.reshape(n_y, half, width - ny * cut), ('yh', 'yl'), 0, 0...]
  transfers between devices with their start and end apart: 15 -> 17, of which waited for: 9 -> 12; matrix products, arithmetic and copies ran while one was open for 6% -> 6% of each run, Pallas kernels for 0% -> 0%
where the time goes in v4:
time: 208 us; the launch traced here: 207 us
  blocking collectives  63.5 us (31%)
  waiting for transfers between devices  45.5 us (22%)
  starting transfers between devices  32.3 us (16%)
  Pallas kernels  30.1 us (14%)
  between operations  15.7 us (8%)
  other arithmetic  12.8 us (6%)
  local copies, waits for them, and re-layouts  7.13 us (3%)
    all_to_all x1, blocking collectives, spread(): return lax.all_to_all(wide, axes, 0, 0, tiled=True)  36.5 us
    pallas_call x1, Pallas kernels, on_device(): pl.pallas_call(functools.partial(block_kernel, low), out_shape=[*sums, *s...  30.1 us
    ppermute x9, waiting for transfers between devices, over(): part = lax.ppermute(part, axes, [(i, (i + k) % n) for i in range(n)])  15.6 us
    all_to_all x1, blocking collectives, on_device(): one = lax.all_to_all(one.reshape(nz, per * 8, LANE), 'z', 0, 0, tiled=True)  15 us
    ppermute x9, starting transfers between devices, over(): part = lax.ppermute(part, axes, [(i, (i + k) % n) for i in range(n)])  13.8 us
    all_to_all x1, waiting for transfers between devices, spread(): return lax.all_to_all(wide, axes, 0, 0, tiled=True)  12 us
    all_to_all x1, blocking collectives, on_device(): lax.all_to_all(split, T, 0, 0, tiled=True).transpose(1, 0, 2)  11.9 us
    all_gather x1, waiting for transfers between devices, on_device(): packed = lax.all_gather(packed, PLANE, axis=0)  10.6 us
  transfers between devices with their start and end apart: 17, of which 12 were waited for; matrix products, arithmetic and copies ran while one was open for 6% of the time, Pallas kernels for 0%

profile of v4, /device:TPU:1, one launch (start us, length us, event | category | flops | bytes accessed | tf_op | source)
XLA Modules:
  0.0 207.1 jit_solution(7525200107902703458)
XLA Ops:
  7.2 1.0 broadcast_select_fusion
  8.9 0.8 copy.25
  9.9 11.9 %all_to_all.25 = bf16[8,64,144]{2,1,0:T(8,128)(2,1)S(1)} all-to-all(bf16[8,64,144]{2,1,0:T(8,128)(2,1)S(1)} %bitcast.100), channel_id=1, replica_groups=mesh['z'=8,'yh'=2,'core'=2,'yl'=2,'x'=4] {'yl','x'}, dimensions={0} | all-to-all | bytes 294912 | tf_op jit(solution)/shard_map/all_to_all | solution.py:217
  22.0 0.3 broadcast_in_dim.23
  22.4 36.5 %all_to_all.26 = bf16[8,64,1152]{2,1,0:T(8,128)(2,1)S(1)} all-to-all(bf16[8,64,1152]{2,1,0:T(8,128)(2,1)S(1)} %broadcast_in_dim.24), channel_id=1, replica_groups=mesh['z'=8,'yh'=2,'core'=2,'yl'=2,'x'=4] {'z'}, dimensions={0} | all-to-all | bytes 2359296 | tf_op jit(solution)/shard_map/all_to_all | solution.py:24
  58.9 4.0 %collective-permute-start = (bf16[512,1152]{1,0:T(8,128)(2,1)S(1)}, bf16[512,1152]{1,0:T(8,128)(2,1)S(1)}, u32[]{:S(2)}, u32[]{:S(2)}) collective-permute-start(bf16[512,1152]{1,0:T(8,128)(2,1)S(1)} %bitcast.97), channel_id=1, source_target_pairs={{0,8},{8,0},{1,9},{9,1},{2,10},{10,2},{3,11},{11,3},{4,12},{12,4},... | collective-permute-start | bytes 3538952 | tf_op jit(solution)/shard_map/ppermute | solution.py:219
  64.2 0.6 pad_maximum_fusion.5.scalars
  64.7 0.6 pad_add_fusion.1.info
  65.3 0.6 pad_add_fusion
  65.9 10.6 %all-gather.3.cloned.1.call-done = bf16[144,144,128]{2,1,0:T(8,128)(2,1)} async-done(((bf16[9,144,128]{2,1,0:T(8,128)(2,1)}), bf16[144,144,128]{2,1,0:T(8,128)(2,1)}) %all-gather.3.cloned.1.call-update) | async-done | bytes 5308432 | tf_op jit(solution)/shard_map/all_gather | solution.py:214
  76.6 2.0 slice.48
  78.6 0.9 collective-permute-start.1
  79.5 5.1 %collective-permute-done.1.other = bf16[16,5,144,128]{3,2,1,0:T(8,128)(2,1)} collective-permute-done((bf16[16,5,144,128]{3,2,1,0:T(8,128)(2,1)S(1)}, bf16[16,5,144,128]{3,2,1,0:T(8,128)(2,1)}, u32[]{:S(2)}, u32[]{:S(2)}) %collective-permute-start.1) | collective-permute-done | bytes 2949152 | tf_op jit(solution)/shard_map/ppermute | solution.py:230
  84.7 30.1 %block.1 = (bf16[2,1152,384]{2,1,0:T(8,128)(2,1)}, bf16[1152,384]{1,0:T(8,128)(2,1)}, bf16[2,1152,384]{2,1,0:T(8,128)(2,1)}, bf16[1152,384]{1,0:T(8,128)(2,1)}, f32[1,1024]{1,0:T(1,128)}) custom-call(s32[3]{0:T(128)} %pad_add_fusion.1.info, f32[3]{0:T(128)} %pad_maximum_fusion.5.scalars, s32[1,1024]{1,0:T(1,128)} %bitcast.120, ...), custom_call_target="tpu_custom_call" | custom-call | flops 18119393280 | bytes 20971520 | tf_op jit(solution)/shard_map/block/pallas_call | solution.py:241
  114.8 0.5 collective-permute-start.2
  115.3 0.5 broadcast.71
  115.8 1.3 reduce.4
  117.4 1.4 collective-permute-done.2
  118.8 1.9 add_convert_fusion
  120.8 1.4 pad_maximum_fusion
  122.2 3.9 %all-to-all-start.2 = ((bf16[4,584,384]{2,1,0:T(8,128)(2,1)}), bf16[4,584,384]{2,1,0:T(8,128)(2,1)S(1)}, u32[]{:S(2)}, u32[]{:S(2)}) async-start(bf16[4,584,384]{2,1,0:T(8,128)(2,1)} %pad_maximum_fusion), calls=%async_computation.2 | async-start | bytes 3588096 | tf_op jit(solution)/shard_map/all_to_all | solution.py:303
  126.1 0.9 copy-done.1
  127.0 1.7 add_convert_fusion.1
  128.7 0.9 dynamic-slice_bitcast_fusion.2
  129.6 0.8 collective-permute-start.7
  130.4 2.4 %collective-permute-start.8 = (bf16[2,144,384]{2,1,0:T(8,128)(2,1)}, bf16[2,144,384]{2,1,0:T(8,128)(2,1)S(1)}, u32[]{:S(2)}, u32[]{:S(2)}) collective-permute-start(bf16[2,144,384]{2,1,0:T(8,128)(2,1)} %get-tuple-element.34), channel_id=1, source_target_pairs={{0,2},{1,3},{2,0},{3,1},{4,6},{5,7},{6,4},{7,5},{8,10},{9,11},{10,... | collective-permute-start | bytes 663560 | tf_op jit(solution)/shard_map/ppermute | solution.py:293
  132.8 1.2 collective-permute-start.9
  134.0 3.3 %collective-permute-done.7 = bf16[2,144,384]{2,1,0:T(8,128)(2,1)S(1)} collective-permute-done((bf16[2,144,384]{2,1,0:T(8,128)(2,1)}, bf16[2,144,384]{2,1,0:T(8,128)(2,1)S(1)}, u32[]{:S(2)}, u32[]{:S(2)}) %collective-permute-start.7) | collective-permute-done | bytes 221216 | tf_op jit(solution)/shard_map/ppermute | solution.py:293
  137.3 5.6 %collective-permute-done.8 = bf16[2,144,384]{2,1,0:T(8,128)(2,1)S(1)} collective-permute-done((bf16[2,144,384]{2,1,0:T(8,128)(2,1)}, bf16[2,144,384]{2,1,0:T(8,128)(2,1)S(1)}, u32[]{:S(2)}, u32[]{:S(2)}) %collective-permute-start.8) | collective-permute-done | bytes 221216 | tf_op jit(solution)/shard_map/ppermute | solution.py:293
  142.9 1.1 fusion.2
  144.1 1.2 collective-permute-start.10
  145.3 2.4 %collective-permute-start.11 = (bf16[72,384]{1,0:T(8,128)(2,1)S(1)}, bf16[72,384]{1,0:T(8,128)(2,1)S(1)}, u32[]{:S(2)}, u32[]{:S(2)}) collective-permute-start(bf16[72,384]{1,0:T(8,128)(2,1)S(1)} %get-tuple-element.43), channel_id=1, source_target_pairs={{0,16},{4,20},{16,0},{20,4},{1,17},{5,21},{17,1},{21,5},{2,18},{6,... | collective-permute-start | bytes 165896 | tf_op jit(solution)/shard_map/ppermute | solution.py:293
  147.7 1.2 collective-permute-start.12
  148.9 2.2 %collective-permute-done.10 = bf16[72,384]{1,0:T(8,128)(2,1)S(1)} collective-permute-done((bf16[72,384]{1,0:T(8,128)(2,1)S(1)}, bf16[72,384]{1,0:T(8,128)(2,1)S(1)}, u32[]{:S(2)}, u32[]{:S(2)}) %collective-permute-start.10) | collective-permute-done | bytes 55328 | tf_op jit(solution)/shard_map/ppermute | solution.py:293
  151.3 0.3 convert_reduce_fusion
  151.8 2.0 collective-permute-start.3
  153.8 2.6 %collective-permute-start.4 = (bf16[152,384]{1,0:T(8,128)(2,1)S(1)}, bf16[152,384]{1,0:T(8,128)(2,1)S(1)}, u32[]{:S(2)}, u32[]{:S(2)}) collective-permute-start(bf16[152,384]{1,0:T(8,128)(2,1)S(1)} %get-tuple-element.45), channel_id=1, source_target_pairs={{0,2},{1,3},{2,0},{3,1},{4,6},{5,7},{6,4},{7,5},{8,10},{9,11},{10,... | collective-permute-start | bytes 350216 | tf_op jit(solution)/shard_map/ppermute | solution.py:293
  156.4 1.0 collective-permute-done.3
  157.4 2.5 %collective-permute-done.4 = bf16[152,384]{1,0:T(8,128)(2,1)S(1)} collective-permute-done((bf16[152,384]{1,0:T(8,128)(2,1)S(1)}, bf16[152,384]{1,0:T(8,128)(2,1)S(1)}, u32[]{:S(2)}, u32[]{:S(2)}) %collective-permute-start.4) | collective-permute-done | bytes 116768 | tf_op jit(solution)/shard_map/ppermute | solution.py:293
  159.9 0.8 collective-permute-done.5
  160.8 15.0 %all_to_all.27 = bf16[8,88,128]{2,1,0:T(8,128)(2,1)S(1)} all-to-all(bf16[8,88,128]{2,1,0:T(8,128)(2,1)S(1)} %bitcast.108), channel_id=1, replica_groups=mesh['z'=8,'yh'=2,'core'=2,'yl'=2,'x'=4] {'z'}, dimensions={0} | all-to-all | bytes 360448 | tf_op jit(solution)/shard_map/all_to_all | solution.py:332
  175.9 0.8 broadcast_in_dim.28
  176.6 3.5 %all-to-all-start.4 = ((bf16[16,88,128]{2,1,0:T(8,128)(2,1)}), bf16[16,88,128]{2,1,0:T(8,128)(2,1)S(1)}, u32[]{:S(2)}, u32[]{:S(2)}) async-start(bf16[16,88,128]{2,1,0:T(8,128)(2,1)} %broadcast_in_dim.28), calls=%async_computation.4 | async-start | bytes 720896 | tf_op jit(solution)/shard_map/all_to_all | solution.py:24
  180.2 12.0 %all-to-all-done.4 = bf16[16,88,128]{2,1,0:T(8,128)(2,1)S(1)} async-done(((bf16[16,88,128]{2,1,0:T(8,128)(2,1)}), bf16[16,88,128]{2,1,0:T(8,128)(2,1)S(1)}, u32[]{:S(2)}, u32[]{:S(2)}) %all-to-all-start.4) | async-done | bytes 360480 | tf_op jit(solution)/shard_map/all_to_all | solution.py:24
  192.3 5.5 %collective-permute-start.13 = (bf16[144,1152]{1,0:T(8,128)(2,1)S(1)}, bf16[144,1152]{1,0:T(8,128)(2,1)S(1)}, u32[]{:S(2)}, u32[]{:S(2)}) collective-permute-start(bf16[144,1152]{1,0:T(8,128)(2,1)S(1)} %maximum_maximum_fusion), channel_id=1, source_target_pairs={{0,8},{8,0},{1,9},{9,1},{2,10},{10,2},{3,11},{11,3},{4,12},{12,4},... | collective-permute-start | bytes 995336 | tf_op jit(solution)/shard_map/ppermute | solution.py:339
  197.8 0.6 broadcast_multiply_fusion
  198.4 0.7 collective-permute-done.13
  199.1 1.2 select_convert_fusion
  (57 shorter events, 2.1 us)
Async XLA Ops:
  7.2 1.3 copy-start.3
  7.2 69.4 %all-gather.3.cloned.1.call-start = ((), (), s32[]{:S(2)}) async-start(), calls=%async_computation.5 | async-start | bytes 5640192 | tf_op jit(solution)/shard_map/all_gather | solution.py:214
  8.5 1.2 copy-start.2
  58.9 19.7 %copy-start = (bf16[8,64,1152]{2,1,0:T(8,128)(2,1)}, bf16[8,64,1152]{2,1,0:T(8,128)(2,1)S(1)}, u32[]{:S(2)}) copy-start(bf16[8,64,1152]{2,1,0:T(8,128)(2,1)S(1)} %all_to_all.26) | copy-start | bytes 3538948
  58.9 7.0 %collective-permute-start = (bf16[512,1152]{1,0:T(8,128)(2,1)S(1)}, bf16[512,1152]{1,0:T(8,128)(2,1)S(1)}, u32[]{:S(2)}, u32[]{:S(2)}) collective-permute-start(bf16[512,1152]{1,0:T(8,128)(2,1)S(1)} %bitcast.97), channel_id=1, source_target_pairs={{0,8},{8,0},{1,9},{9,1},{2,10},{10,2},{3,11},{11,3},{4,12},{12,4},... | collective-permute-start | bytes 3538952 | tf_op jit(solution)/shard_map/ppermute | solution.py:219
  65.9 12.7 %copy-start.4 = (bf16[512,1152]{1,0:T(8,128)(2,1)}, bf16[512,1152]{1,0:T(8,128)(2,1)S(1)}, u32[]{:S(2)}) copy-start(bf16[512,1152]{1,0:T(8,128)(2,1)S(1)} %collective-permute-done.text_b) | copy-start | bytes 3538948
  78.6 6.1 %collective-permute-start.1 = (bf16[16,5,144,128]{3,2,1,0:T(8,128)(2,1)S(1)}, bf16[16,5,144,128]{3,2,1,0:T(8,128)(2,1)}, u32[]{:S(2)}, u32[]{:S(2)}) collective-permute-start(bf16[16,5,144,128]{3,2,1,0:T(8,128)(2,1)S(1)} %slice.48), channel_id=1, source_target_pairs={{0,8},{8,0},{1,9},{9,1},{2,10},{10,2},{3,11},{11,3},{4,12},{12,4},... | collective-permute-start | bytes 8847368 | tf_op jit(solution)/shard_map/ppermute | solution.py:230
  114.8 4.0 %collective-permute-start.2 = (bf16[2,1152,384]{2,1,0:T(8,128)(2,1)}, bf16[2,1152,384]{2,1,0:T(8,128)(2,1)S(1)}, u32[]{:S(2)}, u32[]{:S(2)}) collective-permute-start(bf16[2,1152,384]{2,1,0:T(8,128)(2,1)} %get-tuple-element.25), channel_id=1, source_target_pairs={{0,8},{8,0},{1,9},{9,1},{2,10},{10,2},{3,11},{11,3},{4,12},{12,4},... | collective-permute-start | bytes 5308424 | tf_op jit(solution)/shard_map/ppermute | solution.py:298
  117.2 9.0 %collective-permute-start.6 = (bf16[1152,384]{1,0:T(8,128)(2,1)}, bf16[1152,384]{1,0:T(8,128)(2,1)S(1)}, u32[]{:S(2)}, u32[]{:S(2)}) collective-permute-start(bf16[1152,384]{1,0:T(8,128)(2,1)} %get-tuple-element.28), channel_id=1, source_target_pairs={{0,8},{8,0},{1,9},{9,1},{2,10},{10,2},{3,11},{11,3},{4,12},{12,4},... | collective-permute-start | bytes 2654216 | tf_op jit(solution)/shard_map/ppermute | solution.py:298
  122.2 29.1 %all-to-all-start.2 = ((bf16[4,584,384]{2,1,0:T(8,128)(2,1)}), bf16[4,584,384]{2,1,0:T(8,128)(2,1)S(1)}, u32[]{:S(2)}, u32[]{:S(2)}) async-start(bf16[4,584,384]{2,1,0:T(8,128)(2,1)} %pad_maximum_fusion), calls=%async_computation.2 | async-start | bytes 3588096 | tf_op jit(solution)/shard_map/all_to_all | solution.py:303
  126.1 0.9 copy-start.1
  129.6 7.7 %collective-permute-start.7 = (bf16[2,144,384]{2,1,0:T(8,128)(2,1)}, bf16[2,144,384]{2,1,0:T(8,128)(2,1)S(1)}, u32[]{:S(2)}, u32[]{:S(2)}) collective-permute-start(bf16[2,144,384]{2,1,0:T(8,128)(2,1)} %get-tuple-element.32), channel_id=1, source_target_pairs={{0,1},{1,2},{2,3},{3,0},{4,5},{5,6},{6,7},{7,4},{8,9},{9,10},{10,1... | collective-permute-start | bytes 663560 | tf_op jit(solution)/shard_map/ppermute | solution.py:293
  130.4 12.5 %collective-permute-start.8 = (bf16[2,144,384]{2,1,0:T(8,128)(2,1)}, bf16[2,144,384]{2,1,0:T(8,128)(2,1)S(1)}, u32[]{:S(2)}, u32[]{:S(2)}) collective-permute-start(bf16[2,144,384]{2,1,0:T(8,128)(2,1)} %get-tuple-element.34), channel_id=1, source_target_pairs={{0,2},{1,3},{2,0},{3,1},{4,6},{5,7},{6,4},{7,5},{8,10},{9,11},{10,... | collective-permute-start | bytes 663560 | tf_op jit(solution)/shard_map/ppermute | solution.py:293
  132.8 10.1 %collective-permute-start.9 = (bf16[2,144,384]{2,1,0:T(8,128)(2,1)S(1)}, bf16[2,144,384]{2,1,0:T(8,128)(2,1)}, u32[]{:S(2)}, u32[]{:S(2)}) collective-permute-start(bf16[2,144,384]{2,1,0:T(8,128)(2,1)S(1)} %get-tuple-element.33), channel_id=1, source_target_pairs={{0,3},{1,0},{2,1},{3,2},{4,7},{5,4},{6,5},{7,6},{8,11},{9,8},{10,9... | collective-permute-start | bytes 663560 | tf_op jit(solution)/shard_map/ppermute | solution.py:293
  144.1 7.0 %collective-permute-start.10 = (bf16[72,384]{1,0:T(8,128)(2,1)S(1)}, bf16[72,384]{1,0:T(8,128)(2,1)S(1)}, u32[]{:S(2)}, u32[]{:S(2)}) collective-permute-start(bf16[72,384]{1,0:T(8,128)(2,1)S(1)} %get-tuple-element.41), channel_id=1, source_target_pairs={{0,4},{4,16},{16,20},{20,0},{1,5},{5,17},{17,21},{21,1},{2,6},{6,1... | collective-permute-start | bytes 165896 | tf_op jit(solution)/shard_map/ppermute | solution.py:293
  145.3 5.8 %collective-permute-start.11 = (bf16[72,384]{1,0:T(8,128)(2,1)S(1)}, bf16[72,384]{1,0:T(8,128)(2,1)S(1)}, u32[]{:S(2)}, u32[]{:S(2)}) collective-permute-start(bf16[72,384]{1,0:T(8,128)(2,1)S(1)} %get-tuple-element.43), channel_id=1, source_target_pairs={{0,16},{4,20},{16,0},{20,4},{1,17},{5,21},{17,1},{21,5},{2,18},{6,... | collective-permute-start | bytes 165896 | tf_op jit(solution)/shard_map/ppermute | solution.py:293
  147.7 3.6 %collective-permute-start.12 = (bf16[72,384]{1,0:T(8,128)(2,1)S(1)}, bf16[72,384]{1,0:T(8,128)(2,1)S(1)}, u32[]{:S(2)}, u32[]{:S(2)}) collective-permute-start(bf16[72,384]{1,0:T(8,128)(2,1)S(1)} %get-tuple-element.42), channel_id=1, source_target_pairs={{0,20},{4,0},{16,4},{20,16},{1,21},{5,1},{17,5},{21,17},{2,22},{6,... | collective-permute-start | bytes 165896 | tf_op jit(solution)/shard_map/ppermute | solution.py:293
  151.8 5.5 %collective-permute-start.3 = (bf16[152,384]{1,0:T(8,128)(2,1)S(1)}, bf16[152,384]{1,0:T(8,128)(2,1)S(1)}, u32[]{:S(2)}, u32[]{:S(2)}) collective-permute-start(bf16[152,384]{1,0:T(8,128)(2,1)S(1)} %get-tuple-element.44), channel_id=1, source_target_pairs={{0,1},{1,2},{2,3},{3,0},{4,5},{5,6},{6,7},{7,4},{8,9},{9,10},{10,1... | collective-permute-start | bytes 350216 | tf_op jit(solution)/shard_map/ppermute | solution.py:293
  153.8 6.1 %collective-permute-start.4 = (bf16[152,384]{1,0:T(8,128)(2,1)S(1)}, bf16[152,384]{1,0:T(8,128)(2,1)S(1)}, u32[]{:S(2)}, u32[]{:S(2)}) collective-permute-start(bf16[152,384]{1,0:T(8,128)(2,1)S(1)} %get-tuple-element.45), channel_id=1, source_target_pairs={{0,2},{1,3},{2,0},{3,1},{4,6},{5,7},{6,4},{7,5},{8,10},{9,11},{10,... | collective-permute-start | bytes 350216 | tf_op jit(solution)/shard_map/ppermute | solution.py:293
  156.4 4.3 %collective-permute-start.5 = (bf16[152,384]{1,0:T(8,128)(2,1)S(1)}, bf16[152,384]{1,0:T(8,128)(2,1)S(1)}, u32[]{:S(2)}, u32[]{:S(2)}) collective-permute-start(bf16[152,384]{1,0:T(8,128)(2,1)S(1)} %get-tuple-element.46), channel_id=1, source_target_pairs={{0,3},{1,0},{2,1},{3,2},{4,7},{5,4},{6,5},{7,6},{8,11},{9,8},{10,9... | collective-permute-start | bytes 350216 | tf_op jit(solution)/shard_map/ppermute | solution.py:293
  176.6 15.6 %all-to-all-start.4 = ((bf16[16,88,128]{2,1,0:T(8,128)(2,1)}), bf16[16,88,128]{2,1,0:T(8,128)(2,1)S(1)}, u32[]{:S(2)}, u32[]{:S(2)}) async-start(bf16[16,88,128]{2,1,0:T(8,128)(2,1)} %broadcast_in_dim.28), calls=%async_computation.4 | async-start | bytes 720896 | tf_op jit(solution)/shard_map/all_to_all | solution.py:24
  192.3 6.7 %collective-permute-start.13 = (bf16[144,1152]{1,0:T(8,128)(2,1)S(1)}, bf16[144,1152]{1,0:T(8,128)(2,1)S(1)}, u32[]{:S(2)}, u32[]{:S(2)}) collective-permute-start(bf16[144,1152]{1,0:T(8,128)(2,1)S(1)} %maximum_maximum_fusion), channel_id=1, source_target_pairs={{0,8},{8,0},{1,9},{9,1},{2,10},{10,2},{3,11},{11,3},{4,12},{12,4},... | collective-permute-start | bytes 995336 | tf_op jit(solution)/shard_map/ppermute | solution.py:339
Sparse Core Ops, SparseCore 0:
  11.0 65.4 all-gather.2

commit v5 on v4

--- a/solution.py
+++ b/solution.py
@@ -233,7 +233,7 @@
     smem = pl.BlockSpec(memory_space=pltpu.SMEM)
     vmem = pl.BlockSpec(memory_space=pltpu.VMEM)
     hbm = pl.BlockSpec(memory_space=pl.ANY)
-    cut = width // LANE // 3 * LANE
+    cut = width // LANE // 4 * LANE
     sums = [
         jax.ShapeDtypeStruct((ny, full, cut), BF),
         jax.ShapeDtypeStruct((full, width - ny * cut), BF),

time: 208 us -> 206 us (level)
  blocking collectives: 63.5 us -> 79.3 us
  waiting for transfers between devices: 45.5 us -> 35.6 us
  starting transfers between devices: 32.3 us -> 26.3 us
    all_to_all x1 -> x2, blocking collectives: 36.5 us -> 52.3 us  [spread(): return lax.all_to_all(wide, axes, 0, 0, tiled=True)]
    all_to_all x1 -> x0, waiting for transfers between devices: 12 us -> none  [spread(): return lax.all_to_all(wide, axes, 0, 0, tiled=True)]
    all_to_all x1 -> x0, starting transfers between devices: 3.55 us -> none  [spread(): return lax.all_to_all(wide, axes, 0, 0, tiled=True)]
    ppermute x9, starting transfers between devices: 13.8 us -> 11.6 us  [over(): part = lax.ppermute(part, axes, [(i, (i + k) % n) for i in range(n)])]
  transfers between devices with their start and end apart: 17 -> 16, of which waited for: 12 -> 9; matrix products, arithmetic and copies ran while one was open for 6% -> 6% of each run, Pallas kernels for 0% -> 0%
where the time goes in v5:
time: 206 us; the launch traced here: 205 us
  blocking collectives  79.3 us (38%)
  waiting for transfers between devices  35.6 us (17%)
  Pallas kernels  30.2 us (15%)
  starting transfers between devices  26.3 us (13%)
  between operations  15.7 us (8%)
  other arithmetic  12.5 us (6%)
  local copies, waits for them, and re-layouts  5.51 us (3%)
    all_to_all x2, blocking collectives, spread(): return lax.all_to_all(wide, axes, 0, 0, tiled=True)  52.3 us
    pallas_call x1, Pallas kernels, on_device(): pl.pallas_call(functools.partial(block_kernel, low), out_shape=[*sums, *s...  30.2 us
    ppermute x9, waiting for transfers between devices, over(): part = lax.ppermute(part, axes, [(i, (i + k) % n) for i in range(n)])  17.3 us
    all_to_all x1, blocking collectives, on_device(): one = lax.all_to_all(one.reshape(nz, per * 8, LANE), 'z', 0, 0, tiled=True)  15.1 us
    all_to_all x1, blocking collectives, on_device(): lax.all_to_all(split, T, 0, 0, tiled=True).transpose(1, 0, 2)  11.9 us
    ppermute x9, starting transfers between devices, over(): part = lax.ppermute(part, axes, [(i, (i + k) % n) for i in range(n)])  11.6 us
    all_gather x1, waiting for transfers between devices, on_device(): packed = lax.all_gather(packed, PLANE, axis=0)  10.6 us
    ppermute x1, starting transfers between devices, on_device(): two = lax.ppermute(one, 'core', SWAP)  5.62 us
  transfers between devices with their start and end apart: 16, of which 9 were waited for; matrix products, arithmetic and copies ran while one was open for 6% of the time, Pallas kernels for 0%

profile of v5, /device:TPU:1, one launch (start us, length us, event | category | flops | bytes accessed | tf_op | source)
XLA Modules:
  0.0 205.1 jit_solution(17594930358862150078)
XLA Ops:
  7.2 1.0 broadcast_select_fusion
  8.3 0.2 reshape.96
  8.6 0.2 pad_maximum_fusion.1
  8.9 0.8 copy.25
  9.9 11.9 %all_to_all.25 = bf16[8,64,144]{2,1,0:T(8,128)(2,1)S(1)} all-to-all(bf16[8,64,144]{2,1,0:T(8,128)(2,1)S(1)} %bitcast.103), channel_id=1, replica_groups=mesh['z'=8,'yh'=2,'core'=2,'yl'=2,'x'=4] {'yl','x'}, dimensions={0} | all-to-all | bytes 294912 | tf_op jit(solution)/shard_map/all_to_all | solution.py:217
  21.8 0.1 copy.27
  22.0 0.3 broadcast_in_dim.23
  22.4 36.5 %all_to_all.26 = bf16[8,64,1152]{2,1,0:T(8,128)(2,1)S(1)} all-to-all(bf16[8,64,1152]{2,1,0:T(8,128)(2,1)S(1)} %broadcast_in_dim.24), channel_id=1, replica_groups=mesh['z'=8,'yh'=2,'core'=2,'yl'=2,'x'=4] {'z'}, dimensions={0} | all-to-all | bytes 2359296 | tf_op jit(solution)/shard_map/all_to_all | solution.py:24
  58.9 4.0 %collective-permute-start = (bf16[512,1152]{1,0:T(8,128)(2,1)S(1)}, bf16[512,1152]{1,0:T(8,128)(2,1)S(1)}, u32[]{:S(2)}, u32[]{:S(2)}) collective-permute-start(bf16[512,1152]{1,0:T(8,128)(2,1)S(1)} %bitcast.100), channel_id=1, source_target_pairs={{0,8},{8,0},{1,9},{9,1},{2,10},{10,2},{3,11},{11,3},{4,12},{12,4},... | collective-permute-start | bytes 3538952 | tf_op jit(solution)/shard_map/ppermute | solution.py:219
  64.2 0.6 pad_maximum_fusion.5.scalars
  64.8 0.6 pad_add_fusion.1.info
  65.4 0.6 pad_add_fusion
  66.0 10.6 %all-gather.3.cloned.1.call-done = bf16[144,144,128]{2,1,0:T(8,128)(2,1)} async-done(((bf16[9,144,128]{2,1,0:T(8,128)(2,1)}), bf16[144,144,128]{2,1,0:T(8,128)(2,1)}) %all-gather.3.cloned.1.call-update) | async-done | bytes 5308432 | tf_op jit(solution)/shard_map/all_gather | solution.py:214
  76.6 2.0 slice.42
  78.6 0.9 collective-permute-start.1
  79.5 5.1 %collective-permute-done.1.other = bf16[16,5,144,128]{3,2,1,0:T(8,128)(2,1)} collective-permute-done((bf16[16,5,144,128]{3,2,1,0:T(8,128)(2,1)S(1)}, bf16[16,5,144,128]{3,2,1,0:T(8,128)(2,1)}, u32[]{:S(2)}, u32[]{:S(2)}) %collective-permute-start.1) | collective-permute-done | bytes 2949152 | tf_op jit(solution)/shard_map/ppermute | solution.py:230
  84.7 30.2 %block.1 = (bf16[2,1152,256]{2,1,0:T(8,128)(2,1)}, bf16[1152,640]{1,0:T(8,128)(2,1)}, bf16[2,1152,256]{2,1,0:T(8,128)(2,1)}, bf16[1152,640]{1,0:T(8,128)(2,1)}, f32[1,1024]{1,0:T(1,128)}) custom-call(s32[3]{0:T(128)} %pad_add_fusion.1.info, f32[3]{0:T(128)} %pad_maximum_fusion.5.scalars, s32[1,1024]{1,0:T(1,128)} %bitcast.120, ...), custom_call_target="tpu_custom_call" | custom-call | flops 18119393280 | bytes 20971520 | tf_op jit(solution)/shard_map/block/pallas_call | solution.py:241
  114.8 0.5 collective-permute-start.6
  115.5 0.5 broadcast.71
  116.0 1.3 reduce.4
  117.4 2.0 collective-permute-done.6
  119.4 1.7 add_convert_fusion
  121.1 0.9 dynamic-slice_bitcast_fusion.2
  122.0 1.2 collective-permute-start.7
  123.2 2.4 %collective-permute-start.8 = (bf16[2,144,640]{2,1,0:T(8,128)(2,1)S(1)}, bf16[2,144,640]{2,1,0:T(8,128)(2,1)}, u32[]{:S(2)}, u32[]{:S(2)}) collective-permute-start(bf16[2,144,640]{2,1,0:T(8,128)(2,1)S(1)} %get-tuple-element.31), channel_id=1, source_target_pairs={{0,2},{1,3},{2,0},{3,1},{4,6},{5,7},{6,4},{7,5},{8,10},{9,11},{10,... | collective-permute-start | bytes 1105928 | tf_op jit(solution)/shard_map/ppermute | solution.py:293
  125.6 1.2 collective-permute-start.9
  126.8 1.6 add_convert_fusion.1
  128.4 1.1 pad_maximum_fusion
  129.5 3.5 %all-to-all-start.2 = ((bf16[4,584,256]{2,1,0:T(8,128)(2,1)}), bf16[4,584,256]{2,1,0:T(8,128)(2,1)S(1)}, u32[]{:S(2)}, u32[]{:S(2)}) async-start(bf16[4,584,256]{2,1,0:T(8,128)(2,1)} %pad_maximum_fusion), calls=%async_computation.2 | async-start | bytes 2392064 | tf_op jit(solution)/shard_map/all_to_all | solution.py:303
  133.0 0.3 collective-permute-done.7
  133.3 8.8 %collective-permute-done.8 = bf16[2,144,640]{2,1,0:T(8,128)(2,1)} collective-permute-done((bf16[2,144,640]{2,1,0:T(8,128)(2,1)S(1)}, bf16[2,144,640]{2,1,0:T(8,128)(2,1)}, u32[]{:S(2)}, u32[]{:S(2)}) %collective-permute-start.8) | collective-permute-done | bytes 368672 | tf_op jit(solution)/shard_map/ppermute | solution.py:293
  142.1 1.4 fusion.2
  143.6 0.4 collective-permute-start.10
  144.0 2.4 %collective-permute-start.11 = (bf16[72,640]{1,0:T(8,128)(2,1)S(1)}, bf16[72,640]{1,0:T(8,128)(2,1)S(1)}, u32[]{:S(2)}, u32[]{:S(2)}) collective-permute-start(bf16[72,640]{1,0:T(8,128)(2,1)S(1)} %get-tuple-element.39), channel_id=1, source_target_pairs={{0,16},{4,20},{16,0},{20,4},{1,17},{5,21},{17,1},{21,5},{2,18},{6,... | collective-permute-start | bytes 276488 | tf_op jit(solution)/shard_map/ppermute | solution.py:293
  146.5 1.2 collective-permute-start.12
  147.6 5.1 %collective-permute-done.10 = bf16[72,640]{1,0:T(8,128)(2,1)S(1)} collective-permute-done((bf16[72,640]{1,0:T(8,128)(2,1)S(1)}, bf16[72,640]{1,0:T(8,128)(2,1)S(1)}, u32[]{:S(2)}, u32[]{:S(2)}) %collective-permute-start.10) | collective-permute-done | bytes 92192 | tf_op jit(solution)/shard_map/ppermute | solution.py:293
  152.8 0.2 convert_reduce_fusion
  153.2 0.3 collective-permute-start.3
  153.5 2.3 %collective-permute-start.4 = (bf16[152,256]{1,0:T(8,128)(2,1)S(1)}, bf16[152,256]{1,0:T(8,128)(2,1)S(1)}, u32[]{:S(2)}, u32[]{:S(2)}) collective-permute-start(bf16[152,256]{1,0:T(8,128)(2,1)S(1)} %get-tuple-element.45), channel_id=1, source_target_pairs={{0,2},{1,3},{2,0},{3,1},{4,6},{5,7},{6,4},{7,5},{8,10},{9,11},{10,... | collective-permute-start | bytes 233480 | tf_op jit(solution)/shard_map/ppermute | solution.py:293
  155.8 0.2 collective-permute-start.5
  156.0 2.5 %collective-permute-done.3 = bf16[152,256]{1,0:T(8,128)(2,1)S(1)} collective-permute-done((bf16[152,256]{1,0:T(8,128)(2,1)S(1)}, bf16[152,256]{1,0:T(8,128)(2,1)S(1)}, u32[]{:S(2)}, u32[]{:S(2)}) %collective-permute-start.3) | collective-permute-done | bytes 77856 | tf_op jit(solution)/shard_map/ppermute | solution.py:293
  158.6 0.6 collective-permute-done.5
  159.2 15.1 %all_to_all.27 = bf16[8,88,128]{2,1,0:T(8,128)(2,1)S(1)} all-to-all(bf16[8,88,128]{2,1,0:T(8,128)(2,1)S(1)} %bitcast.108), channel_id=1, replica_groups=mesh['z'=8,'yh'=2,'core'=2,'yl'=2,'x'=4] {'z'}, dimensions={0} | all-to-all | bytes 360448 | tf_op jit(solution)/shard_map/all_to_all | solution.py:332
  174.4 15.7 %all_to_all.28 = bf16[16,88,128]{2,1,0:T(8,128)(2,1)S(1)} all-to-all(bf16[16,88,128]{2,1,0:T(8,128)(2,1)S(1)} %broadcast_in_dim.28), channel_id=1, replica_groups=mesh['z'=8,'yh'=2,'core'=2,'yl'=2,'x'=4] {'z','yh'}, dimensions={0} | all-to-all | bytes 720896 | tf_op jit(solution)/shard_map/all_to_all | solution.py:24
  190.2 5.6 %collective-permute-start.13 = (bf16[144,1152]{1,0:T(8,128)(2,1)S(1)}, bf16[144,1152]{1,0:T(8,128)(2,1)S(1)}, u32[]{:S(2)}, u32[]{:S(2)}) collective-permute-start(bf16[144,1152]{1,0:T(8,128)(2,1)S(1)} %maximum_maximum_fusion), channel_id=1, source_target_pairs={{0,8},{8,0},{1,9},{9,1},{2,10},{10,2},{3,11},{11,3},{4,12},{12,4},... | collective-permute-start | bytes 995336 | tf_op jit(solution)/shard_map/ppermute | solution.py:339
  195.9 0.6 broadcast_multiply_fusion
  196.5 0.6 collective-permute-done.13
  197.1 1.2 select_convert_fusion
  (56 shorter events, 1.2 us)
Async XLA Ops:
  7.2 1.3 copy-start.3
  7.2 69.4 %all-gather.3.cloned.1.call-start = ((), (), s32[]{:S(2)}) async-start(), calls=%async_computation.5 | async-start | bytes 5640192 | tf_op jit(solution)/shard_map/all_gather | solution.py:214
  8.5 1.2 copy-start.2
  58.9 19.7 %copy-start.1 = (bf16[8,64,1152]{2,1,0:T(8,128)(2,1)}, bf16[8,64,1152]{2,1,0:T(8,128)(2,1)S(1)}, u32[]{:S(2)}) copy-start(bf16[8,64,1152]{2,1,0:T(8,128)(2,1)S(1)} %all_to_all.26) | copy-start | bytes 3538948
  58.9 7.1 %collective-permute-start = (bf16[512,1152]{1,0:T(8,128)(2,1)S(1)}, bf16[512,1152]{1,0:T(8,128)(2,1)S(1)}, u32[]{:S(2)}, u32[]{:S(2)}) collective-permute-start(bf16[512,1152]{1,0:T(8,128)(2,1)S(1)} %bitcast.100), channel_id=1, source_target_pairs={{0,8},{8,0},{1,9},{9,1},{2,10},{10,2},{3,11},{11,3},{4,12},{12,4},... | collective-permute-start | bytes 3538952 | tf_op jit(solution)/shard_map/ppermute | solution.py:219
  66.0 12.6 %copy-start.4 = (bf16[512,1152]{1,0:T(8,128)(2,1)}, bf16[512,1152]{1,0:T(8,128)(2,1)S(1)}, u32[]{:S(2)}) copy-start(bf16[512,1152]{1,0:T(8,128)(2,1)S(1)} %collective-permute-done.text_b) | copy-start | bytes 3538948
  78.6 6.1 %collective-permute-start.1 = (bf16[16,5,144,128]{3,2,1,0:T(8,128)(2,1)S(1)}, bf16[16,5,144,128]{3,2,1,0:T(8,128)(2,1)}, u32[]{:S(2)}, u32[]{:S(2)}) collective-permute-start(bf16[16,5,144,128]{3,2,1,0:T(8,128)(2,1)S(1)} %slice.42), channel_id=1, source_target_pairs={{0,8},{8,0},{1,9},{9,1},{2,10},{10,2},{3,11},{11,3},{4,12},{12,4},... | collective-permute-start | bytes 8847368 | tf_op jit(solution)/shard_map/ppermute | solution.py:230
  114.8 4.5 %collective-permute-start.6 = (bf16[1152,640]{1,0:T(8,128)(2,1)}, bf16[1152,640]{1,0:T(8,128)(2,1)S(1)}, u32[]{:S(2)}, u32[]{:S(2)}) collective-permute-start(bf16[1152,640]{1,0:T(8,128)(2,1)} %get-tuple-element.28), channel_id=1, source_target_pairs={{0,8},{8,0},{1,9},{9,1},{2,10},{10,2},{3,11},{11,3},{4,12},{12,4},... | collective-permute-start | bytes 4423688 | tf_op jit(solution)/shard_map/ppermute | solution.py:298
  115.3 11.4 %collective-permute-start.2 = (bf16[2,1152,256]{2,1,0:T(8,128)(2,1)}, bf16[2,1152,256]{2,1,0:T(8,128)(2,1)}, u32[]{:S(2)}, u32[]{:S(2)}) collective-permute-start(bf16[2,1152,256]{2,1,0:T(8,128)(2,1)} %get-tuple-element.25), channel_id=1, source_target_pairs={{0,8},{8,0},{1,9},{9,1},{2,10},{10,2},{3,11},{11,3},{4,12},{12,4},... | collective-permute-start | bytes 3538952 | tf_op jit(solution)/shard_map/ppermute | solution.py:298
  121.1 5.7 %copy-start = (bf16[2,1152,256]{2,1,0:T(8,128)(2,1)S(1)}, bf16[2,1152,256]{2,1,0:T(8,128)(2,1)}, u32[]{:S(2)}) copy-start(bf16[2,1152,256]{2,1,0:T(8,128)(2,1)} %get-tuple-element.24) | copy-start | bytes 3538948
  122.0 11.3 %collective-permute-start.7 = (bf16[2,144,640]{2,1,0:T(8,128)(2,1)}, bf16[2,144,640]{2,1,0:T(8,128)(2,1)}, u32[]{:S(2)}, u32[]{:S(2)}) collective-permute-start(bf16[2,144,640]{2,1,0:T(8,128)(2,1)} %get-tuple-element.29), channel_id=1, source_target_pairs={{0,1},{1,2},{2,3},{3,0},{4,5},{5,6},{6,7},{7,4},{8,9},{9,10},{10,1... | collective-permute-start | bytes 1105928 | tf_op jit(solution)/shard_map/ppermute | solution.py:293
  123.2 19.0 %collective-permute-start.8 = (bf16[2,144,640]{2,1,0:T(8,128)(2,1)S(1)}, bf16[2,144,640]{2,1,0:T(8,128)(2,1)}, u32[]{:S(2)}, u32[]{:S(2)}) collective-permute-start(bf16[2,144,640]{2,1,0:T(8,128)(2,1)S(1)} %get-tuple-element.31), channel_id=1, source_target_pairs={{0,2},{1,3},{2,0},{3,1},{4,6},{5,7},{6,4},{7,5},{8,10},{9,11},{10,... | collective-permute-start | bytes 1105928 | tf_op jit(solution)/shard_map/ppermute | solution.py:293
  125.6 16.6 %collective-permute-start.9 = (bf16[2,144,640]{2,1,0:T(8,128)(2,1)S(1)}, bf16[2,144,640]{2,1,0:T(8,128)(2,1)}, u32[]{:S(2)}, u32[]{:S(2)}) collective-permute-start(bf16[2,144,640]{2,1,0:T(8,128)(2,1)S(1)} %get-tuple-element.30), channel_id=1, source_target_pairs={{0,3},{1,0},{2,1},{3,2},{4,7},{5,4},{6,5},{7,6},{8,11},{9,8},{10,9... | collective-permute-start | bytes 1105928 | tf_op jit(solution)/shard_map/ppermute | solution.py:293
  129.5 23.3 %all-to-all-start.2 = ((bf16[4,584,256]{2,1,0:T(8,128)(2,1)}), bf16[4,584,256]{2,1,0:T(8,128)(2,1)S(1)}, u32[]{:S(2)}, u32[]{:S(2)}) async-start(bf16[4,584,256]{2,1,0:T(8,128)(2,1)} %pad_maximum_fusion), calls=%async_computation.2 | async-start | bytes 2392064 | tf_op jit(solution)/shard_map/all_to_all | solution.py:303
  143.6 9.1 %collective-permute-start.10 = (bf16[72,640]{1,0:T(8,128)(2,1)S(1)}, bf16[72,640]{1,0:T(8,128)(2,1)S(1)}, u32[]{:S(2)}, u32[]{:S(2)}) collective-permute-start(bf16[72,640]{1,0:T(8,128)(2,1)S(1)} %get-tuple-element.37), channel_id=1, source_target_pairs={{0,4},{4,16},{16,20},{20,0},{1,5},{5,17},{17,21},{21,1},{2,6},{6,1... | collective-permute-start | bytes 276488 | tf_op jit(solution)/shard_map/ppermute | solution.py:293
  144.0 8.7 %collective-permute-start.11 = (bf16[72,640]{1,0:T(8,128)(2,1)S(1)}, bf16[72,640]{1,0:T(8,128)(2,1)S(1)}, u32[]{:S(2)}, u32[]{:S(2)}) collective-permute-start(bf16[72,640]{1,0:T(8,128)(2,1)S(1)} %get-tuple-element.39), channel_id=1, source_target_pairs={{0,16},{4,20},{16,0},{20,4},{1,17},{5,21},{17,1},{21,5},{2,18},{6,... | collective-permute-start | bytes 276488 | tf_op jit(solution)/shard_map/ppermute | solution.py:293
  146.5 6.3 %collective-permute-start.12 = (bf16[72,640]{1,0:T(8,128)(2,1)S(1)}, bf16[72,640]{1,0:T(8,128)(2,1)S(1)}, u32[]{:S(2)}, u32[]{:S(2)}) collective-permute-start(bf16[72,640]{1,0:T(8,128)(2,1)S(1)} %get-tuple-element.38), channel_id=1, source_target_pairs={{0,20},{4,0},{16,4},{20,16},{1,21},{5,1},{17,5},{21,17},{2,22},{6,... | collective-permute-start | bytes 276488 | tf_op jit(solution)/shard_map/ppermute | solution.py:293
  153.2 5.4 %collective-permute-start.3 = (bf16[152,256]{1,0:T(8,128)(2,1)S(1)}, bf16[152,256]{1,0:T(8,128)(2,1)S(1)}, u32[]{:S(2)}, u32[]{:S(2)}) collective-permute-start(bf16[152,256]{1,0:T(8,128)(2,1)S(1)} %get-tuple-element.44), channel_id=1, source_target_pairs={{0,1},{1,2},{2,3},{3,0},{4,5},{5,6},{6,7},{7,4},{8,9},{9,10},{10,1... | collective-permute-start | bytes 233480 | tf_op jit(solution)/shard_map/ppermute | solution.py:293
  153.5 5.0 %collective-permute-start.4 = (bf16[152,256]{1,0:T(8,128)(2,1)S(1)}, bf16[152,256]{1,0:T(8,128)(2,1)S(1)}, u32[]{:S(2)}, u32[]{:S(2)}) collective-permute-start(bf16[152,256]{1,0:T(8,128)(2,1)S(1)} %get-tuple-element.45), channel_id=1, source_target_pairs={{0,2},{1,3},{2,0},{3,1},{4,6},{5,7},{6,4},{7,5},{8,10},{9,11},{10,... | collective-permute-start | bytes 233480 | tf_op jit(solution)/shard_map/ppermute | solution.py:293
  155.8 3.3 %collective-permute-start.5 = (bf16[152,256]{1,0:T(8,128)(2,1)S(1)}, bf16[152,256]{1,0:T(8,128)(2,1)S(1)}, u32[]{:S(2)}, u32[]{:S(2)}) collective-permute-start(bf16[152,256]{1,0:T(8,128)(2,1)S(1)} %get-tuple-element.46), channel_id=1, source_target_pairs={{0,3},{1,0},{2,1},{3,2},{4,7},{5,4},{6,5},{7,6},{8,11},{9,8},{10,9... | collective-permute-start | bytes 233480 | tf_op jit(solution)/shard_map/ppermute | solution.py:293
  190.2 6.9 %collective-permute-start.13 = (bf16[144,1152]{1,0:T(8,128)(2,1)S(1)}, bf16[144,1152]{1,0:T(8,128)(2,1)S(1)}, u32[]{:S(2)}, u32[]{:S(2)}) collective-permute-start(bf16[144,1152]{1,0:T(8,128)(2,1)S(1)} %maximum_maximum_fusion), channel_id=1, source_target_pairs={{0,8},{8,0},{1,9},{9,1},{2,10},{10,2},{3,11},{11,3},{4,12},{12,4},... | collective-permute-start | bytes 995336 | tf_op jit(solution)/shard_map/ppermute | solution.py:339
Sparse Core Ops, SparseCore 0:
  11.0 65.4 all-gather.2
